TPU v7x, 128 devices: a whole 4x4x4 slice. The times are simulated.
128 devices in a mesh: wide: 32 (over x, z_hi, y), narrow: 4 (over z_lo, core).
Axes of the slice: x: 4, y: 4, z: 4 (z_hi: 2, z_lo: 2; z = z_hi * 2 + z_lo), core: 2. Of those that a mesh axis runs over, the one named last changes fastest.
Arguments:
- cube: bfloat16 [16384, 4, 6144], P(('wide', 'narrow')), may hold values from -70 to 70, as said below
- flags: int32 [1024], P(('wide', 'narrow')), may hold values 0 or 1
- line_gain: float32 [8193], replicated, may hold values from 0 to 1
- beam_width: float32 [16384], P(('wide', 'narrow')), may hold values from 1 to 3
Outputs:
- restored: bfloat16 [16384, 4, 6144], P(('wide', 'narrow'))
- continuum: float32 [6, 24576], P(None, ('wide', 'narrow'))
Inputs may be any that keep to these rules, and one draw needn't show every extreme that they name: `cube`: continuum polynomial plus noise per pixel.
All inputs are finite; a program needn't handle non-finite values. No bound on the sum of `flags` on one device may be relied on, other than what follows from the above.
Results may differ from a plain program's by a relative error of at most 0.0049.
Values may be sent and summed in bfloat16 or wider, within the bound.
A program may use at most 192 MiB of HBM per device.

v0:
```python
import jax
import jax.numpy as jnp
from jax import lax
from jax.sharding import PartitionSpec as P

NBASIS = 6
HALF = 8
FLAGBLK = 16


HIGH = lax.Precision.HIGHEST


def legendre(count):
    x = (2.0 * jnp.arange(count, dtype=jnp.float32) + 1.0) / count - 1.0
    terms = [jnp.ones_like(x), x]
    for k in range(1, NBASIS - 1):
        terms.append(((2 * k + 1) * x * terms[k] - k * terms[k - 1]) / (k + 1))
    return jnp.stack(terms[:NBASIS])


def make_taps(widths):
    offsets = jnp.arange(2 * HALF + 1, dtype=jnp.float32) - HALF
    raw = jnp.exp(-offsets[None, :] ** 2 / (2.0 * widths[:, None] ** 2))
    return raw / jnp.sum(raw, axis=1, keepdims=True)


def small_solve(factor, moments):
    count = factor.shape[0]
    inner = []
    for i in range(count):
        value = moments[i]
        for j in range(i):
            value = value - factor[i, j] * inner[j]
        inner.append(value / factor[i, i])
    result = [None] * count
    for i in reversed(range(count)):
        value = inner[i]
        for j in range(i + 1, count):
            value = value - factor[j, i] * result[j]
        result[i] = value / factor[i, i]
    return jnp.stack(result)


def angle_tables(count, other, modulus):
    first_idx = jnp.arange(count, dtype=jnp.int32)[:, None]
    second_idx = jnp.arange(other, dtype=jnp.int32)[None, :]
    phase = (first_idx * second_idx % modulus).astype(jnp.float32) * (2.0 * jnp.pi / modulus)
    return (jnp.cos(phase), jnp.sin(phase))


def spectral_filter(residual, line_gain):
    total, width = residual.shape
    first = 1 << (total.bit_length() - 1) // 2
    second = total // first
    field = residual.reshape(first, second, width)
    cos_a, sin_a = angle_tables(first, first, first)
    cos_b, sin_b = angle_tables(second, second, second)
    turn_c, turn_s = angle_tables(first, second, total)
    turn_c = turn_c[:, :, None]
    turn_s = turn_s[:, :, None]
    real_y = jnp.einsum("ka,abp->kbp", cos_a, field, precision=HIGH)
    imag_y = -jnp.einsum("ka,abp->kbp", sin_a, field, precision=HIGH)
    real_u = real_y * turn_c + imag_y * turn_s
    imag_u = imag_y * turn_c - real_y * turn_s
    real_x = jnp.einsum("kbp,bm->kmp", real_u, cos_b, precision=HIGH) + jnp.einsum(
        "kbp,bm->kmp", imag_u, sin_b, precision=HIGH
    )
    imag_x = jnp.einsum("kbp,bm->kmp", imag_u, cos_b, precision=HIGH) - jnp.einsum(
        "kbp,bm->kmp", real_u, sin_b, precision=HIGH
    )
    bins = (
        jnp.arange(first, dtype=jnp.int32)[:, None]
        + first * jnp.arange(second, dtype=jnp.int32)[None, :]
    )
    gain = line_gain[jnp.minimum(bins, total - bins)][:, :, None]
    real_x = real_x * gain
    imag_x = imag_x * gain
    real_z = jnp.einsum("kmp,mb->kbp", real_x, cos_b, precision=HIGH) - jnp.einsum(
        "kmp,mb->kbp", imag_x, sin_b, precision=HIGH
    )
    imag_z = jnp.einsum("kmp,mb->kbp", imag_x, cos_b, precision=HIGH) + jnp.einsum(
        "kmp,mb->kbp", real_x, sin_b, precision=HIGH
    )
    real_v = real_z * turn_c - imag_z * turn_s
    imag_v = imag_z * turn_c + real_z * turn_s
    result = jnp.einsum("ak,kbp->abp", cos_a, real_v, precision=HIGH) - jnp.einsum(
        "ak,kbp->abp", sin_a, imag_v, precision=HIGH
    )
    return (result / total).reshape(total, width)


def body(cube, flags, line_gain, beam_width):
    ch_dev, rows, npix = cube.shape
    local = cube.reshape(ch_dev, rows * npix)
    all_flags = lax.all_gather(flags, ("wide", "narrow"), axis=0, tiled=True)
    columns = lax.all_to_all(local, ("wide", "narrow"), split_axis=1, concat_axis=0, tiled=True)
    nchan, pix = columns.shape
    basis = legendre(nchan)
    weight = 1.0 - jnp.repeat(all_flags, FLAGBLK).astype(jnp.float32)
    wbasis = basis * weight[None, :]
    gram = jnp.dot(wbasis, basis.T, precision=HIGH)
    factor = jnp.linalg.cholesky(gram)
    y_data = columns.astype(jnp.float32)
    moments = jnp.dot(wbasis, y_data, precision=HIGH)
    coeffs = small_solve(factor, moments)
    smooth = jnp.dot(basis.T, coeffs, precision=HIGH)
    residual = weight[:, None] * (y_data - smooth)
    filtered = spectral_filter(residual, line_gain).astype(jnp.bfloat16)
    back = lax.all_to_all(filtered, ("wide", "narrow"), split_axis=0, concat_axis=1, tiled=True)
    back = back.reshape(ch_dev, rows, npix)
    taps = make_taps(beam_width)
    padded = jnp.pad(back, ((0, 0), (0, 0), (HALF, HALF)))
    summed = jnp.zeros((ch_dev, rows, npix), jnp.float32)
    for j in range(2 * HALF + 1):
        summed = summed + taps[:, None, j : j + 1] * padded[:, :, j : j + npix]
    restored = summed.astype(jnp.bfloat16)
    return (restored, coeffs)


def solution(mesh):
    placed = (P(("wide", "narrow"), None, None), P(("wide", "narrow")), P(), P(("wide", "narrow")))
    return jax.shard_map(
        body,
        mesh=mesh,
        in_specs=placed,
        out_specs=(P(("wide", "narrow"), None, None), P(None, ("wide", "narrow"))),
        check_vma=False,
    )
```

profile of v0, /device:TPU:8, one launch (start us, length us, event | category | flops | bytes accessed | tf_op | source)
XLA Modules:
  0.0 751.3 jit_solution(11811574633174353741)
XLA Ops:
  0.6 0.0 copy-start
  0.6 0.0 copy-start.6
  0.7 11.2 %copy.46 = bf16[128,4,6144]{0,2,1:T(8,128)(2,1)} copy(bf16[128,4,6144]{2,1,0:T(4,128)(2,1)} %param.4) | data formatting | bytes 12582912 | tf_op args[0]
  11.8 10.8 %all-to-all-start = ((bf16[128,128,192]{0,2,1:T(8,128)(2,1)}), bf16[128,128,192]{0,2,1:T(8,128)(2,1)}, u32[]{:S(2)}, u32[]{:S(2)}) async-start(bf16[128,128,192]{0,2,1:T(8,128)(2,1)} %bitcast.161), calls=%async_computation | async-start | bytes 12582912 | tf_op jit(solution)/shard_map/all_to_all | solution.py:97
  22.7 0.0 copy-done.6
  22.7 0.2 dynamic-update-slice.3
  23.0 136.8 %all-reduce.1 = s32[1024]{0:T(1024)S(1)} all-reduce(s32[1024]{0:T(1024)S(1)} %dynamic-update-slice.3), channel_id=1, replica_groups=mesh['wide'=32,'narrow'=4] {'wide','narrow'}, use_global_device_ids=true, to_apply=%add.1 | all-reduce | flops 1024 | bytes 8192
  159.9 0.0 copy-done
  159.9 90.5 %gather_fusion = f32[16384]{0:T(1024)S(1)} fusion(f32[8193]{0:T(1024)S(1)} %copy-done, s32[16384]{0:T(1024)S(1)} %fusion.40), kind=kCustom, calls=%fused_computation | custom fusion | bytes 196608 | tf_op jit(solution)/shard_map/gather | solution.py:76
  250.4 0.1 copy.51
  250.5 0.2 broadcast_in_dim.4
  250.7 0.2 sub.338
  250.9 0.3 broadcast_multiply_fusion.1
  251.2 0.3 multiply_add_fusion.3
  251.5 0.5 subtract_multiply_fusion
  252.1 0.6 stack.4
  252.7 1.2 fusion.29
  254.0 0.1 copy.48
  254.1 0.5 cholesky.18
  254.6 0.1 select_reduce_fusion
  254.7 0.6 compare_reduce_fusion
  255.3 0.6 select_select_fusion
  256.0 0.7 fusion.142
  258.0 0.5 fusion.143
  258.5 0.3 fusion.62
  258.8 0.0 all-to-all-done
  258.8 7.0 fusion.7
  265.8 9.5 %subtract_divide_fusion.6 = (f32[1,192]{1,0:T(1,128)S(1)}, f32[1,192]{1,0:T(1,128)S(1)}, f32[1,192]{1,0:T(1,128)S(1)}, f32[1,192]{1,0:T(1,128)S(1)}, f32[1,192]{1,0:T(1,128)S(1)}) fusion(f32[6,192]{1,0:T(8,128)S(1)} %fusion.7, f32[]{:T(128)} %bitcast.21, f32[]{:T(128)} %bitcast.20, f32[]{:T(128)} %bitcast.19, f32[]{:T(128)} %bitcast.18, f32[]{:T(128)} %bitcast.17, ...), kind=kLoop, calls=%fused_computation.124 | loop fusion | flops 4800 | bytes 7740 | tf_op jit(solution)/shard_map/div | solution.py:35
  275.3 12.6 %subtract_divide_fusion = (f32[1,192]{1,0:T(1,128)S(1)}, f32[1,192]{1,0:T(1,128)S(1)}, f32[1,192]{1,0:T(1,128)S(1)}, f32[1,192]{1,0:T(1,128)S(1)}, f32[1,192]{1,0:T(1,128)S(1)}, /*index=5*/f32[1,192]{1,0:T(1,128)S(1)}) fusion(f32[1,192]{1,0:T(1,128)S(1)} %get-tuple-element.16, f32[]{:T(128)} %bitcast.23, f32[]{:T(128)} %bitcast.18, f32[]{:T(128)} %bitcast.14, ...), kind=kLoop, calls=%fused_computation.118 | loop fusion | flops 8832 | bytes 9300 | tf_op jit(solution)/shard_map/div | solution.py:41
  287.9 0.0 copy-start.5
  287.9 14.4 %fusion.22 = f32[24,8,128,128]{3,1,2,0:T(8,128)} fusion(f32[6,16384]{1,0:T(8,128)S(1)} %stack.4, f32[6,192]{1,0:T(8,128)S(1)} %stack.5, f32[16384]{0:T(1024)S(1)} %sub.338, bf16[128,128,192]{0,2,1:T(8,128)(2,1)} %all-to-all-done), kind=kOutput, calls=%fused_computation.36 | convolution fusion | flops 235929600 | bytes 19337728 | tf_op jit(solution)/shard_map/dot_general | solution.py:107
  302.3 11.5 %copy.93 = f32[24,8,128,128]{3,2,1,0:T(8,128)} copy(f32[24,8,128,128]{3,1,2,0:T(8,128)} %fusion.22) | data formatting | bytes 25165824
  313.8 0.0 copy-done.5
  313.8 0.0 copy-start.2
  313.8 18.9 %fusion.46 = f32[128,128,192]{1,0,2:T(8,128)} fusion(f32[128,128,192]{1,0,2:T(8,128)} %bitcast.155), kind=kOutput, calls=%fused_computation.66 | convolution fusion | flops 4832067584 | bytes 25165824 | tf_op jit(solution)/shard_map/ka,abp->kbp/dot_general | solution.py:63
  332.7 0.0 copy-done.2
  332.7 14.0 %fusion.53 = f32[128,128,192]{1,0,2:T(8,128)} fusion(f32[128,128,192]{1,0,2:T(8,128)S(1)} %bitcast.156), kind=kOutput, calls=%fused_computation.73 | convolution fusion | flops 4832067584 | bytes 25165824 | tf_op jit(solution)/shard_map/ka,abp->kbp/dot_general | solution.py:62
  346.7 21.2 %fusion.25 = f32[128,128,192]{1,0,2:T(8,128)} fusion(f32[128,128,192]{1,0,2:T(8,128)} %fusion.53, f32[128,128,192]{1,0,2:T(8,128)} %fusion.46, f32[128,128]{1,0:T(8,128)S(1)} %get-tuple-element.59, f32[128,128]{1,0:T(8,128)S(1)} %get-tuple-element.60), kind=kOutput, calls=%fused_computation.39 | convolution fusion | flops 4844650496 | bytes 37879808 | tf_op jit(solution)/shard_map/kbp,bm->kmp/dot_general | solution.py:69
  367.9 21.2 %fusion.23 = f32[128,128,192]{1,0,2:T(8,128)} fusion(f32[128,128,192]{1,0,2:T(8,128)} %fusion.53, f32[128,128,192]{1,0,2:T(8,128)} %fusion.46, f32[128,128]{1,0:T(8,128)S(1)} %get-tuple-element.59, f32[128,128]{1,0:T(8,128)S(1)} %get-tuple-element.60), kind=kOutput, calls=%fused_computation.37 | convolution fusion | flops 4844650496 | bytes 37879808 | tf_op jit(solution)/shard_map/kbp,bm->kmp/dot_general | solution.py:69
  389.2 26.0 %fusion.20 = f32[128,128,192]{0,1,2:T(8,128)} fusion(f32[128,128,192]{1,0,2:T(8,128)} %fusion.25, f32[128,128,192]{1,0,2:T(8,128)} %fusion.23, f32[128,128]{0,1:T(8,128)S(1)} %copy.51), kind=kOutput, calls=%fused_computation.34 | convolution fusion | flops 4838359040 | bytes 37814272 | tf_op jit(solution)/shard_map/kmp,mb->kbp/dot_general | solution.py:82
  415.2 0.0 slice-done.3
  415.2 0.0 slice-done.4
  415.2 0.0 slice-done.5
  415.2 0.0 copy-done.4
  415.2 23.3 %fusion.21 = f32[128,128,192]{0,1,2:T(8,128)} fusion(f32[128,128,192]{1,0,2:T(8,128)S(1)} %bitcast.160, f32[128,128,192]{1,0,2:T(8,128)S(1)} %copy-done.4, f32[128,128]{0,1:T(8,128)S(1)} %copy.51), kind=kOutput, calls=%fused_computation.35 | convolution fusion | flops 4838359040 | bytes 37814272 | tf_op jit(solution)/shard_map/kmp,mb->kbp/dot_general | solution.py:79
  438.5 21.5 %fusion.26 = f32[128,128,192]{1,0,2:T(8,128)} fusion(f32[128,128,192]{1,0,2:T(8,128)} %fusion.53, f32[128,128,192]{1,0,2:T(8,128)} %fusion.46, f32[128,128]{1,0:T(8,128)S(1)} %get-tuple-element.59, f32[128,128]{1,0:T(8,128)S(1)} %get-tuple-element.60), kind=kOutput, calls=%fused_computation.40 | convolution fusion | flops 4844650496 | bytes 37879808 | tf_op jit(solution)/shard_map/kbp,bm->kmp/dot_general | solution.py:66
  460.0 21.1 %fusion.24 = f32[128,128,192]{1,0,2:T(8,128)} fusion(f32[128,128,192]{1,0,2:T(8,128)} %fusion.53, f32[128,128,192]{1,0,2:T(8,128)} %fusion.46, f32[128,128]{1,0:T(8,128)S(1)} %get-tuple-element.59, f32[128,128]{1,0:T(8,128)S(1)} %get-tuple-element.60), kind=kOutput, calls=%fused_computation.38 | convolution fusion | flops 4844650496 | bytes 37879808 | tf_op jit(solution)/shard_map/kbp,bm->kmp/dot_general | solution.py:66
  481.1 27.2 %fusion.18 = f32[128,128,192]{0,1,2:T(8,128)} fusion(f32[128,128,192]{1,0,2:T(8,128)} %fusion.24, f32[128,128,192]{1,0,2:T(8,128)} %fusion.26, f32[128,128]{0,1:T(8,128)S(1)} %copy.51), kind=kOutput, calls=%fused_computation.32 | convolution fusion | flops 4838359040 | bytes 37814272 | tf_op jit(solution)/shard_map/kmp,mb->kbp/dot_general | solution.py:82
  508.3 0.0 slice-done
  508.3 0.0 slice-done.1
  508.3 0.0 slice-done.2
  508.3 0.0 copy-done.3
  508.3 23.1 %fusion.19 = f32[128,128,192]{0,1,2:T(8,128)} fusion(f32[128,128,192]{1,0,2:T(8,128)S(1)} %copy-done.3, f32[128,128,192]{1,0,2:T(8,128)S(1)} %bitcast.158, f32[128,128]{0,1:T(8,128)S(1)} %copy.51), kind=kOutput, calls=%fused_computation.33 | convolution fusion | flops 4838359040 | bytes 37814272 | tf_op jit(solution)/shard_map/kmp,mb->kbp/dot_general | solution.py:79
  531.4 25.9 %fusion.2 = f32[128,128,192]{1,0,2:T(8,128)} fusion(f32[128,128]{1,0:T(8,128)S(1)} %get-tuple-element.59, f32[128,128]{1,0:T(8,128)S(1)} %get-tuple-element.60, f32[128,128,192]{0,1,2:T(8,128)} %fusion.20, f32[128,128,192]{0,1,2:T(8,128)} %fusion.18, f32[128,128,192]{0,1,2:T(8,128)} %fusion.19, f32[128,128,192]{0,1,2:T(8,128)} %fusion.21), kind=kOutput, calls=%fused_computation.6 | convolution fusion | flops 4847796224 | bytes 63045632 | tf_op jit(solution)/shard_map/ak,kbp->abp/dot_general | solution.py:87
  557.3 27.6 %multiply_convert_fusion = bf16[128,128,192]{1,0,2:T(8,128)(2,1)} fusion(f32[128,128,192]{1,0,2:T(8,128)} %fusion.2, f32[128,128]{1,0:T(8,128)S(1)} %get-tuple-element.59, f32[128,128]{1,0:T(8,128)S(1)} %get-tuple-element.60, f32[128,128,192]{0,1,2:T(8,128)} %fusion.20, f32[128,128,192]{0,1,2:T(8,128)} %fusion.18, f32[128,128,192]{0,1,2:T(8,128)} %fusion.19, ...), kind=kOutput, calls=%fused_computation.14 | convolution fusion | flops 4857233408 | bytes 69337088 | tf_op jit(solution)/shard_map/ak,kbp->abp/dot_general | solution.py:87
  584.8 9.5 %copy.66 = bf16[128,128,192]{1,2,0:T(8,128)(2,1)} copy(bf16[128,128,192]{1,0,2:T(8,128)(2,1)} %multiply_convert_fusion) | data formatting | bytes 12582912 | tf_op jit(solution)/shard_map/convert_element_type | solution.py:109
  594.3 6.2 all-to-all-start.1
  600.5 0.0 copy-done.7
  600.5 0.1 fusion.79
  600.6 0.1 fusion.78
  600.7 84.6 %all-to-all-done.1 = bf16[128,128,192]{1,2,0:T(8,128)(2,1)} async-done(((bf16[128,128,192]{1,2,0:T(8,128)(2,1)}), bf16[128,128,192]{1,2,0:T(8,128)(2,1)}, u32[]{:S(2)}, u32[]{:S(2)}) %all-to-all-start.1) | async-done | bytes 6291488 | tf_op jit(solution)/shard_map/all_to_all | solution.py:110
  685.2 54.7 %add_convert_fusion = bf16[128,4,6144]{0,2,1:T(8,128)(2,1)} fusion(bf16[128,4,6144]{0,2,1:T(8,128)(2,1)} %bitcast.42, f32[128]{0:T(128)S(1)} %get-tuple-element.18, f32[128]{0:T(128)S(1)} %get-tuple-element.19, f32[128]{0:T(128)S(1)} %get-tuple-element.20, f32[128]{0:T(128)S(1)} %get-tuple-element.21, f32[128]{0:T(128)S(1)} %get-tuple-element.22, ...), kind=kLoop, calls=%fused_computation.13 | loop fusion | flops 160432128 | bytes 12591616 | tf_op jit(solution)/shard_map/convert_element_type | solution.py:117
  739.9 11.2 %copy.67 = bf16[128,4,6144]{2,1,0:T(4,128)(2,1)} copy(bf16[128,4,6144]{0,2,1:T(8,128)(2,1)} %add_convert_fusion) | data formatting | bytes 12582912
  751.1 0.0 copy-done.1
  (22 shorter events, 0.2 us)
Async XLA Ops:
  0.6 159.2 %copy-start = (f32[8193]{0:T(1024)S(1)}, f32[8193]{0:T(1024)}, u32[]{:S(2)}) copy-start(f32[8193]{0:T(1024)} %param.6) | copy-start | bytes 98320
  0.6 22.1 %copy-start.6 = (s32[8]{0:T(128)S(1)}, s32[8]{0:T(128)}, u32[]{:S(2)}) copy-start(s32[8]{0:T(128)} %param.5) | copy-start | bytes 100
  11.8 247.0 %all-to-all-start = ((bf16[128,128,192]{0,2,1:T(8,128)(2,1)}), bf16[128,128,192]{0,2,1:T(8,128)(2,1)}, u32[]{:S(2)}, u32[]{:S(2)}) async-start(bf16[128,128,192]{0,2,1:T(8,128)(2,1)} %bitcast.161), calls=%async_computation | async-start | bytes 12582912 | tf_op jit(solution)/shard_map/all_to_all | solution.py:97
  287.9 25.9 %copy-start.5 = (f32[6,192]{1,0:T(8,128)}, f32[6,192]{1,0:T(8,128)S(1)}, u32[]{:S(2)}) copy-start(f32[6,192]{1,0:T(8,128)S(1)} %stack.5) | copy-start | bytes 13828
  313.8 18.9 %copy-start.2 = (f32[24,8,128,128]{3,2,1,0:T(8,128)S(1)}, f32[24,8,128,128]{3,2,1,0:T(8,128)}, u32[]{:S(2)}) copy-start(f32[24,8,128,128]{3,2,1,0:T(8,128)} %copy.93) | copy-start | bytes 37748740
  367.9 47.3 %slice-start.3 = ((s8[12582912]{0:T(1024)(128)(4,1)}), s8[4194304]{0:T(1024)(128)(4,1)S(1)}, s32[]{:S(2)}) async-start(s8[12582912]{0:T(1024)(128)(4,1)} %bitcast.159), calls=%async_computation.5 | async-start | bytes 8388608
  367.9 47.3 %slice-start.4 = ((s8[12582912]{0:T(1024)(128)(4,1)}), s8[4194304]{0:T(1024)(128)(4,1)S(1)}, s32[]{:S(2)}) async-start(s8[12582912]{0:T(1024)(128)(4,1)} %bitcast.159), calls=%async_computation.6 | async-start | bytes 8388608
  389.2 26.0 %slice-start.5 = ((s8[12582912]{0:T(1024)(128)(4,1)}), s8[4194304]{0:T(1024)(128)(4,1)S(1)}, s32[]{:S(2)}) async-start(s8[12582912]{0:T(1024)(128)(4,1)} %bitcast.159), calls=%async_computation.7 | async-start | bytes 8388608
  389.2 26.0 %copy-start.4 = (f32[128,128,192]{1,0,2:T(8,128)S(1)}, f32[128,128,192]{1,0,2:T(8,128)}, u32[]{:S(2)}) copy-start(f32[128,128,192]{1,0,2:T(8,128)} %fusion.23) | copy-start | bytes 37748740
  460.0 48.3 %slice-start = ((s8[12582912]{0:T(1024)(128)(4,1)}), s8[4194304]{0:T(1024)(128)(4,1)S(1)}, s32[]{:S(2)}) async-start(s8[12582912]{0:T(1024)(128)(4,1)} %bitcast.157), calls=%async_computation.2 | async-start | bytes 8388608
  460.0 48.3 %slice-start.1 = ((s8[12582912]{0:T(1024)(128)(4,1)}), s8[4194304]{0:T(1024)(128)(4,1)S(1)}, s32[]{:S(2)}) async-start(s8[12582912]{0:T(1024)(128)(4,1)} %bitcast.157), calls=%async_computation.3 | async-start | bytes 8388608
  481.1 27.2 %slice-start.2 = ((s8[12582912]{0:T(1024)(128)(4,1)}), s8[4194304]{0:T(1024)(128)(4,1)S(1)}, s32[]{:S(2)}) async-start(s8[12582912]{0:T(1024)(128)(4,1)} %bitcast.157), calls=%async_computation.4 | async-start | bytes 8388608
  481.1 27.2 %copy-start.3 = (f32[128,128,192]{1,0,2:T(8,128)S(1)}, f32[128,128,192]{1,0,2:T(8,128)}, u32[]{:S(2)}) copy-start(f32[128,128,192]{1,0,2:T(8,128)} %fusion.24) | copy-start | bytes 37748740
  584.8 15.6 %copy-start.7 = (f32[128]{0:T(128)S(1)}, f32[128]{0:T(128)}, u32[]{:S(2)}) copy-start(f32[128]{0:T(128)} %param.7) | copy-start | bytes 1540
  594.3 90.9 %all-to-all-start.1 = ((bf16[128,128,192]{1,2,0:T(8,128)(2,1)}), bf16[128,128,192]{1,2,0:T(8,128)(2,1)}, u32[]{:S(2)}, u32[]{:S(2)}) async-start(bf16[128,128,192]{1,2,0:T(8,128)(2,1)} %copy.66), calls=%async_computation.1 | async-start | bytes 12582912 | tf_op jit(solution)/shard_map/all_to_all | solution.py:110
  685.2 65.9 %copy-start.1 = (f32[8193]{0:T(1024)S(1)}, f32[8193]{0:T(1024)}, u32[]{:S(2)}) copy-start(f32[8193]{0:T(1024)} %param.6) | copy-start | bytes 98320
where the time goes:
time: 761 us; the launch traced here: 751 us
  matrix products  294 us (39%)
  local copies, waits for them, and re-layouts  137 us (18%)
  blocking collectives  137 us (18%)
  waiting for transfers between devices  84.6 us (11%)
  other arithmetic  80.3 us (11%)
  starting transfers between devices  17 us (2%)
    unnamed x1, blocking collectives  137 us
    gather x2, local copies, waits for them, and re-layouts, spectral_filter(): gain = line_gain[jnp.minimum(bins, total - bins)][:, :, None]  90.6 us
    all_to_all x1, waiting for transfers between devices, body(): lax.all_to_all(filtered, ('wide', 'narrow'), split_axis=0, concat_axis=1,...  84.6 us
    convert_element_type x1, other arithmetic, body(): restored = summed.astype(jnp.bfloat16)  54.7 us
    unnamed x33, local copies, waits for them, and re-layouts  34.2 us
    dot_general x1, matrix products, spectral_filter(): jnp.einsum('ak,kbp->abp', sin_a, imag_v, precision=HIGH)  27.6 us
    dot_general x1, matrix products, spectral_filter(): jnp.einsum('kmp,mb->kbp', real_x, sin_b, precision=HIGH)  27.2 us
    dot_general x1, matrix products, spectral_filter(): jnp.einsum('kmp,mb->kbp', imag_x, cos_b, precision=HIGH)  26 us
  transfers between devices with their start and end apart: 2, of which 1 were waited for; matrix products, arithmetic and copies ran while one was open for 13% of the time, Pallas kernels for 0%

commit v1 on v0

v1 whole, which is shorter than its diff:
```python
import functools
import math

import jax
import jax.numpy as jnp
import numpy as np
from jax import lax
from jax.experimental import pallas as pl
from jax.experimental.pallas import tpu as pltpu
from jax.sharding import PartitionSpec as P

NDEV = 128
NBASIS = 6
HALF = 8
FLAGBLK = 16
ROWS = 4
NPIX = 6144
NCHAN = 16384
SIDE = 128
HROWS = 72
OWN = NPIX // NDEV
GROUP = 16
FLAGGED = 128.0
LIMIT = 100.0
BF = jnp.bfloat16
F32 = jnp.float32
VMEM_BYTES = 56 * 1024 * 1024
AXES = ("wide", "narrow")


def split3(x):
    hi = x.astype(BF)
    rest = x - hi.astype(np.float64)
    lo = rest.astype(BF)
    return hi, lo, (rest - lo.astype(np.float64)).astype(BF)


def legendre64(x):
    terms = [np.ones_like(x), x]
    for k in range(1, NBASIS - 1):
        terms.append(((2 * k + 1) * x * terms[k] - k * terms[k - 1]) / (k + 1))
    return np.stack(terms[:NBASIS])


@functools.cache
def tables():
    idx = np.arange(SIDE)
    turn = 2.0 * np.pi / SIDE
    half = SIDE // 2 + 1
    cos = np.cos(turn * (np.outer(idx, idx) % SIDE))
    sin = np.sin(turn * (np.outer(idx, idx) % SIDE))
    first = np.zeros((2 * HROWS, SIDE))
    first[:half] = cos[:half]
    first[HROWS : HROWS + half] = -sin[:half]
    plain = first.astype(np.float32)
    slow = legendre64((2.0 * idx + 1.0) / SIDE - 1.0)
    first[half : half + NBASIS] = slow
    fa_hi, fa_lo, fa_rest = split3(first)
    fa_hi = fa_hi.copy()
    fa_hi[HROWS + half : HROWS + half + NBASIS] = fa_rest[half : half + NBASIS]
    chan = np.arange(NCHAN)
    full = legendre64((2.0 * chan + 1.0) / NCHAN - 1.0).reshape(NBASIS, SIDE, SIDE)
    fit = np.linalg.pinv(slow.T)
    mix = np.einsum("ma,kab->kmb", fit, full)
    mix = np.where(np.arange(NBASIS)[None, :, None] <= np.arange(NBASIS)[:, None, None], mix, 0.0)
    w2 = np.block([[cos, -sin], [sin, cos]])
    v2 = np.block([[cos, sin], [-sin, cos]])
    times = np.full((half,), 2.0)
    times[0] = times[-1] = 1.0
    last = np.zeros((SIDE, 2 * HROWS))
    last[:, :half] = cos[:, :half] * times
    last[:, HROWS : HROWS + half] = -sin[:, :half] * times
    tc = np.zeros((HROWS, SIDE))
    ts = np.zeros((HROWS, SIDE))
    tc[:half] = np.cos(2.0 * np.pi / NCHAN * np.outer(idx[:half], idx))
    ts[:half] = np.sin(2.0 * np.pi / NCHAN * np.outer(idx[:half], idx))
    w_hi, w_lo, _ = split3(w2)
    v_hi, v_lo, _ = split3(v2)
    l_hi, l_lo, _ = split3(last)
    f = np.float32
    return dict(
        fa=np.stack([fa_hi, fa_lo]), plain=plain, full=full.astype(f), mix=mix.astype(f),
        w2=np.stack([w_hi, w_lo]), v2=np.stack([v_hi, v_lo]), last=np.stack([l_hi, l_lo]),
        tc=tc.astype(f), ts=ts.astype(f),
    )


def dot(a, b):
    return jnp.dot(a, b, preferred_element_type=F32)


def halves(x):
    hi = x.astype(BF)
    return hi, (x - hi.astype(F32)).astype(BF)


def dot_right(x, table):
    hi, lo = halves(x)
    return dot(hi, table[0]) + dot(lo, table[0]) + dot(hi, table[1])


def dot_left(table, x):
    hi, lo = halves(x)
    return dot(table[0], hi) + dot(table[0], lo) + dot(table[1], hi)


def unpack_group(src, start, xs):
    @pl.loop(0, SIDE // 8)
    def _(i):
        block = src[pl.ds(i * 8, 8), pl.ds(start, GROUP), :].astype(F32)
        xs[pl.ds(pl.multiple_of(i * 8 * GROUP, 128), 8 * GROUP), :] = block.reshape(8 * GROUP, SIDE)


def pack_group(dst, start, xs):
    @pl.loop(0, SIDE // 8)
    def _(i):
        block = xs[pl.ds(pl.multiple_of(i * 8 * GROUP, 128), 8 * GROUP), :]
        dst[pl.ds(i * 8, 8), pl.ds(start, GROUP), :] = block.reshape(8, GROUP, SIDE).astype(BF)


def fit_setup(xs, full, plain, fw, chol):
    weight = jnp.where(xs[pl.ds(0, SIDE, stride=GROUP), :] > LIMIT, 0.0, 1.0)
    gram = {}
    for i in range(NBASIS):
        weighted = full[i] * weight
        fw[i] = jnp.dot(plain[...], weighted, preferred_element_type=F32, precision=lax.Precision.HIGHEST)
        for j in range(i + 1):
            total = jnp.sum(jnp.sum(weighted * full[j], axis=0, keepdims=True), axis=1, keepdims=True)
            gram[i, j] = jnp.broadcast_to(total, (8, SIDE))
    factor = {}
    for j in range(NBASIS):
        value = gram[j, j]
        for k in range(j):
            value = value - factor[j, k] * factor[j, k]
        factor[j, j] = jnp.sqrt(value)
        for i in range(j + 1, NBASIS):
            value = gram[i, j]
            for k in range(j):
                value = value - factor[i, k] * factor[j, k]
            factor[i, j] = value / factor[j, j]
    for (i, j), value in factor.items():
        chol[i * NBASIS + j] = value


def fit_group(z, tt, mix, chol, cs):
    @pl.loop(0, GROUP)
    def _(p):
        tt[pl.ds(pl.multiple_of(p * 8, 8), 8), :] = z[p, 64:72, :] + z[p, 136:144, :]

    parts = [tt[pl.ds(m + 1, GROUP, stride=8), :] for m in range(NBASIS)]

    def entry(i, j):
        return jnp.broadcast_to(chol[i * NBASIS + j, 0:1, :], (GROUP, SIDE))

    inner = []
    for k in range(NBASIS):
        total = parts[0] * mix[k, 0:1, :]
        for m in range(1, k + 1):
            total = total + parts[m] * mix[k, m : m + 1, :]
        value = jnp.broadcast_to(jnp.sum(total, axis=1, keepdims=True), (GROUP, SIDE))
        for j in range(k):
            value = value - entry(k, j) * inner[j]
        inner.append(value / entry(k, k))
    result = [None] * NBASIS
    for i in reversed(range(NBASIS)):
        value = inner[i]
        for j in range(i + 1, NBASIS):
            value = value - entry(j, i) * result[j]
        result[i] = value / entry(i, i)
    lane = lax.broadcasted_iota(jnp.int32, (GROUP, SIDE), 1)
    shown = jnp.zeros((GROUP, SIDE), F32)
    for k in range(NBASIS):
        cs[k] = result[k]
        shown = jnp.where(lane == k, result[k], shown)
    return shown


def filter_group(xs, z, tt, cs, fa, w2, v2, last, tc, ts, gain, mix, fw, chol):
    @pl.loop(0, GROUP // 2)
    def _(i):
        both = [xs[pl.ds(2 * i + q, SIDE, stride=GROUP), :] for q in range(2)]
        x = jnp.concatenate([jnp.where(v > LIMIT, 0.0, v) for v in both], axis=1).astype(BF)
        res = dot(fa[0], x) + dot(fa[1], x)
        z[2 * i] = res[:, :SIDE]
        z[2 * i + 1] = res[:, SIDE:]

    shown = fit_group(z, tt, mix, chol, cs)
    quad = 4

    @pl.loop(0, GROUP // quad)
    def _(i):
        real, imag = [], []
        for q in range(quad):
            p = i * quad + q
            zr, zi = z[p, :HROWS, :], z[p, HROWS:, :]
            for k in range(NBASIS):
                coef = cs[k, pl.ds(p, 1), :]
                zr = zr - coef * fw[k, :HROWS, :]
                zi = zi - coef * fw[k, HROWS:, :]
            real.append(zr * tc[...] + zi * ts[...])
            imag.append(zi * tc[...] - zr * ts[...])
        u = jnp.concatenate([jnp.concatenate(real, axis=0), jnp.concatenate(imag, axis=0)], axis=1)
        x = dot_right(u, w2)
        g = jnp.concatenate([gain[...]] * quad, axis=0)
        x = x * jnp.concatenate([g, g], axis=1)
        v = dot_right(x, v2)
        cols = []
        for q in range(quad):
            vr, vi = v[q * HROWS : (q + 1) * HROWS, :SIDE], v[q * HROWS : (q + 1) * HROWS, SIDE:]
            cols.append(jnp.concatenate([vr * tc[...] - vi * ts[...], vi * tc[...] + vr * ts[...]], axis=0))
        out = dot_left(last, jnp.concatenate(cols, axis=1))
        for q in range(quad):
            xs[pl.ds(i * quad + q, SIDE, stride=GROUP), :] = out[:, q * SIDE : (q + 1) * SIDE]

    return shown


LANES = 512
PARTS = NPIX // LANES
TILES = NPIX // SIDE
TURN = 37


def place():
    wide, narrow = lax.axis_index("wide"), lax.axis_index("narrow")
    return wide, narrow, wide * 4 + narrow


def partner(i):
    wide, narrow, _ = place()
    s = i * TURN % NDEV
    x = (wide // 8 + s % 4) % 4
    y = (wide % 4 + s // 4 % 4) % 4
    z = (wide // 4 % 2 * 2 + narrow // 2 + s // 16 % 4) % 4
    core = (narrow % 2 + s // 64) % 2
    return (x * 2 + z // 2) * 4 + y, z % 2 * 2 + core


def columns(ref, row, device):
    return ref.at[row, pl.ds(pl.multiple_of(device * OWN, 16), OWN)]


def exchange(row, source, target, send_sem, recv_sem):
    @pl.loop(1, NDEV)
    def _(i):
        wide, narrow = partner(i)
        pltpu.make_async_remote_copy(
            src_ref=source(wide * 4 + narrow),
            dst_ref=target,
            send_sem=send_sem.at[row],
            recv_sem=recv_sem.at[row],
            device_id=(wide, narrow),
            device_id_type=pl.DeviceIdType.MESH,
        ).start()


def wait_all(row, buffer, sem):
    block = buffer.at[row, pl.ds(0, NDEV - 1)]
    pltpu.make_async_copy(block, block, sem.at[row]).wait()


def wait_rows(row, buffer, sem):
    block = buffer.at[row, pl.ds(0, (NDEV - 1) * OWN)]
    pltpu.make_async_copy(block, block, sem.at[row]).wait()


def relayout_in(cube_v, work, part):
    lanes = pl.ds(pl.multiple_of(part * LANES, LANES), LANES)
    for c in range(0, SIDE, 16):
        block = cube_v[pl.ds(c, 16), :, lanes].astype(F32).reshape(16 * ROWS, LANES)
        for q in range(LANES // SIDE):
            work[part * (LANES // SIDE) + q, pl.ds(c * ROWS, 16 * ROWS), :] = block[:, q * SIDE : (q + 1) * SIDE]


def relayout_out(cube_v, work, part):
    lanes = pl.ds(pl.multiple_of(part * LANES, LANES), LANES)
    for c in range(0, SIDE, 16):
        parts = [work[part * (LANES // SIDE) + q, pl.ds(c * ROWS, 16 * ROWS), :] for q in range(LANES // SIDE)]
        cube_v[pl.ds(c, 16), :, lanes] = jnp.concatenate(parts, axis=1).reshape(16, ROWS, LANES).astype(BF)


def turn_in(row, tile, work, marks, sent):
    block = work[tile, pl.ds(row, SIDE, stride=ROWS), :]
    turned = jnp.where(marks[...] > 0, FLAGGED, block.T)
    sent[row, pl.ds(pl.multiple_of(tile * SIDE, SIDE), SIDE), :] = turned.astype(BF)


def beam_start(row, back, padded):
    padded[0:HALF, :] = jnp.zeros((HALF, SIDE), F32)
    padded[HALF + NPIX : NPIX + 2 * HALF, :] = jnp.zeros((HALF, SIDE), F32)

    @pl.loop(0, TILES)
    def _(i):
        at = pl.multiple_of(i * SIDE, SIDE)
        padded[pl.ds(at + HALF, SIDE), :] = back[row, pl.ds(at, SIDE), :].astype(F32)


def beam_tile(row, tile, padded, taps, flat, work):
    at = tile * SIDE
    run = SIDE // 8
    values = [padded[pl.ds(at + t, 8, stride=run), :] for t in range(run + 2 * HALF)]
    for t in range(run):
        total = values[t + HALF] * taps[HALF]
        for j in range(HALF):
            total = total + (values[t + j] + values[t + 2 * HALF - j]) * taps[j]
        flat[pl.ds(t, 8, stride=run), :] = total
    work[tile, pl.ds(row, SIDE, stride=ROWS), :] = flat[...].T


def strip_kernel(
    cube, marks, gain, taps, fa, w2, v2, last, tc, ts, mix, full, plain, restored, continuum,
    cube_v, work, sent, got, back, padded, flat, xs, z, tt, cs, fw, chol, shown, gathered,
    in_sem, out_sem, go_send, go_recv, home_send, home_recv, own_sem, fit_send, fit_recv,
):
    my_wide, my_narrow, me = place()

    def cube_part(part):
        lanes = pl.ds(pl.multiple_of(part * LANES, LANES), LANES)
        return pltpu.make_async_copy(cube.at[:, :, lanes], cube_v.at[:, :, lanes], in_sem.at[part])

    def out_part(part):
        lanes = pl.ds(pl.multiple_of(part * LANES, LANES), LANES)
        return pltpu.make_async_copy(cube_v.at[:, :, lanes], restored.at[:, :, lanes], out_sem.at[part])

    def own_go(row):
        return pltpu.make_async_copy(columns(sent, row, me), got.at[row, me], own_sem.at[row])

    def own_home(row):
        return pltpu.make_async_copy(got.at[row, me], columns(back, row, me), own_sem.at[ROWS + row])

    @pl.loop(0, PARTS)
    def _(part):
        cube_part(part).start()

    @pl.loop(0, PARTS)
    def _(part):
        cube_part(part).wait()
        relayout_in(cube_v, work, part)
        for q in range(LANES // SIDE):
            turn_in(0, part * (LANES // SIDE) + q, work, marks, sent)

    for row in range(ROWS):
        if row > 0:
            @pl.loop(0, TILES, step=2)
            def _(tile):
                turn_in(row, tile, work, marks, sent)
                turn_in(row, tile + 1, work, marks, sent)

        own_go(row).start()
        exchange(row, lambda d: columns(sent, row, d), got.at[row, me], go_send, go_recv)

    def fit_target(row):
        return row * (NDEV // ROWS) + me // ROWS

    def fit_remote(row):
        dest = fit_target(row)
        return pltpu.make_async_remote_copy(
            src_ref=shown.at[row],
            dst_ref=gathered.at[me % ROWS],
            send_sem=fit_send.at[row],
            recv_sem=fit_recv.at[me % ROWS],
            device_id=(dest // 4, dest % 4),
            device_id_type=pl.DeviceIdType.MESH,
        )

    def fit_local(row):
        return pltpu.make_async_copy(shown.at[row], gathered.at[me % ROWS], fit_send.at[row])

    for row in range(ROWS):
        own_go(row).wait()
        wait_all(row, got, go_recv)
        rows = got.at[row]
        if row == 0:
            unpack_group(rows, 0, xs)
            fit_setup(xs, full, plain, fw, chol)

        @pl.loop(0, OWN // GROUP)
        def _(g):
            start = pl.multiple_of(g * GROUP, GROUP)
            unpack_group(rows, start, xs)
            shown[row, pl.ds(start, GROUP), :] = filter_group(
                xs, z, tt, cs, fa, w2, v2, last, tc, ts, gain, mix, fw, chol
            )
            pack_group(rows, start, xs)

        own_home(row).start()
        exchange(row, lambda d: got.at[row, d], columns(back, row, me), home_send, home_recv)
        dest = fit_target(row)

        @pl.when(dest != me)
        def _():
            fit_remote(row).start()

        @pl.when(dest == me)
        def _():
            fit_local(row).start()

    for row in range(ROWS):
        own_home(row).wait()
        wait_rows(row, back, home_recv)
        beam_start(row, back, padded)
        if row < ROWS - 1:
            @pl.loop(0, TILES)
            def _(tile):
                beam_tile(row, tile, padded, taps, flat, work)
        else:
            @pl.loop(0, PARTS)
            def _(part):
                for q in range(LANES // SIDE):
                    beam_tile(row, part * (LANES // SIDE) + q, padded, taps, flat, work)
                relayout_out(cube_v, work, part)
                out_part(part).start()

    for row in range(ROWS):
        dest = fit_target(row)

        @pl.when(dest != me)
        def _():
            fit_remote(row).wait_send()

        @pl.when(dest == me)
        def _():
            fit_local(row).wait()

    for slot in range(ROWS):
        source = me % (NDEV // ROWS) * ROWS + slot

        @pl.when(source != me)
        def _():
            block = gathered.at[slot]
            pltpu.make_async_copy(block, block, fit_recv.at[slot]).wait()

    for slot in range(ROWS):
        continuum[slot] = gathered[slot]
    for row in range(ROWS):
        wait_rows(row, sent, go_send)
        wait_all(row, got, home_send)

    @pl.loop(0, PARTS)
    def _(part):
        out_part(part).wait()


def params():
    return pltpu.CompilerParams(vmem_limit_bytes=VMEM_BYTES)


def whole(array):
    return pl.BlockSpec(array.shape, lambda *_: (0,) * array.ndim)


def make_taps(widths):
    offsets = jnp.arange(2 * HALF + 1, dtype=F32) - HALF
    raw = jnp.exp(-offsets[:, None] ** 2 / (2.0 * widths[None, :] ** 2))
    return raw / jnp.sum(raw, axis=0, keepdims=True)


def gain_table(line_gain):
    both = jnp.concatenate([line_gain, line_gain[1:-1][::-1]]) / NCHAN
    return both.reshape(SIDE, SIDE).T[:HROWS]


def body(cube, flags, line_gain, beam_width):
    tab = {k: jnp.asarray(v) for k, v in tables().items()}
    gain = gain_table(line_gain)
    taps = jnp.broadcast_to(make_taps(beam_width)[: HALF + 1, None, :], (HALF + 1, 8, SIDE))
    marks = jnp.repeat(flags, FLAGBLK)[None, :]
    names = ("fa", "w2", "v2", "last", "tc", "ts", "mix", "full", "plain")
    ins = [marks, gain, taps] + [tab[n] for n in names]
    dma = pltpu.SemaphoreType.DMA
    restored, coefs = pl.pallas_call(
        strip_kernel,
        in_specs=[pl.BlockSpec(memory_space=pl.ANY)] + [pl.BlockSpec(memory_space=pltpu.VMEM)] * len(ins),
        out_specs=[pl.BlockSpec(memory_space=pl.ANY), pl.BlockSpec(memory_space=pltpu.VMEM)],
        out_shape=[
            jax.ShapeDtypeStruct((SIDE, ROWS, NPIX), BF),
            jax.ShapeDtypeStruct((ROWS, OWN, SIDE), F32),
        ],
        scratch_shapes=[
            pltpu.VMEM((SIDE, ROWS, NPIX), BF),
            pltpu.VMEM((TILES, SIDE * ROWS, SIDE), F32),
            pltpu.VMEM((ROWS, NPIX, SIDE), BF),
            pltpu.VMEM((ROWS, NDEV, OWN, SIDE), BF),
            pltpu.VMEM((ROWS, NPIX, SIDE), BF),
            pltpu.VMEM((NPIX + 2 * HALF, SIDE), F32),
            pltpu.VMEM((SIDE, SIDE), F32),
            pltpu.VMEM((SIDE * GROUP, SIDE), F32),
            pltpu.VMEM((GROUP, 2 * HROWS, SIDE), F32),
            pltpu.VMEM((GROUP * 8, SIDE), F32),
            pltpu.VMEM((NBASIS, GROUP, SIDE), F32),
            pltpu.VMEM((NBASIS, 2 * HROWS, SIDE), F32),
            pltpu.VMEM((NBASIS * NBASIS, 8, SIDE), F32),
            pltpu.VMEM((ROWS, OWN, SIDE), F32),
            pltpu.VMEM((ROWS, OWN, SIDE), F32),
            dma((PARTS,)),
            dma((PARTS,)),
            dma((ROWS,)),
            dma((ROWS,)),
            dma((ROWS,)),
            dma((ROWS,)),
            dma((2 * ROWS,)),
            dma((ROWS,)),
            dma((ROWS,)),
        ],
        compiler_params=pltpu.CompilerParams(vmem_limit_bytes=VMEM_BYTES, has_side_effects=True),
    )(cube, *ins)
    continuum = coefs.reshape(ROWS * OWN, SIDE)[:, :NBASIS].T
    return (restored, continuum)


def solution(mesh):
    placed = (P(AXES, None, None), P(AXES), P(), P(AXES))
    return jax.shard_map(
        body,
        mesh=mesh,
        in_specs=placed,
        out_specs=(P(AXES, None, None), P(None, AXES)),
        check_vma=False,
    )
```

time: 761 us -> 205 us (0.27)
  the two profiles are of different devices: /device:TPU:8 before, /device:TPU:1 now
where the time goes in v1:
time: 205 us
  Pallas kernels  189 us (92%)
  local copies, waits for them, and re-layouts  13.7 us (7%)
    pallas_call x1, Pallas kernels, body(): pl.pallas_call(strip_kernel, in_specs=[pl.BlockSpec(memory_space=pl.ANY)]...  189 us
    unnamed x4, local copies, waits for them, and re-layouts  10.2 us

profile of v1, /device:TPU:1, one launch (start us, length us, event | category | flops | bytes accessed | tf_op | source)
XLA Modules:
  0.0 204.7 jit_solution(10122973873605836496)
XLA Ops:
  0.6 0.7 multiply_multiply_fusion
  1.3 0.7 broadcast_in_dim.4
  2.0 0.6 broadcast_in_dim_reshape.3.marks
  2.6 0.1 fusion.1
  2.7 0.6 broadcast_in_dim.5.taps
  3.3 0.8 slice.12
  4.2 0.1 reverse
  4.3 0.1 slice.20
  4.3 0.9 fusion
  5.2 0.1 copy.16
  5.3 0.6 slice.16.gain
  5.9 188.7 %shard_map.140 = (bf16[128,4,6144]{2,1,0:T(4,128)(2,1)}, f32[4,48,128]{2,1,0:T(8,128)}) custom-call(bf16[128,4,6144]{2,1,0:T(4,128)(2,1)} %cube.1, s32[1,128]{1,0:T(1,128)} %broadcast_in_dim_reshape.3.marks, f32[72,128]{1,0:T(8,128)} %slice.16.gain, f32[9,8,128]{2,1,0:T(8,128)} %broadcast_in_dim.5.taps, bf16[2,144,128]{2,1,0:T(8,128)(2,1)} %constant.28.clone.fa, ...), custom_call_target="tpu_custom_call" | custom-call | tf_op jit(solution)/shard_map/pallas_call | solution.py:471
  194.7 1.6 copy.18
  196.2 8.5 %copy.20 = bf16[128,4,6144]{2,1,0:T(4,128)(2,1)} copy(bf16[128,4,6144]{2,1,0:T(4,128)(2,1)} %get-tuple-element.10) | data formatting | bytes 12582912
  (2 shorter events, 0.0 us)

commit v2 on v1

--- a/solution.py
+++ b/solution.py
@@ -79,8 +79,8 @@
     l_hi, l_lo, _ = split3(last)
     f = np.float32
     return dict(
-        fa=np.stack([fa_hi, fa_lo]), plain=plain, full=full.astype(f), mix=mix.astype(f),
-        w2=np.stack([w_hi, w_lo]), v2=np.stack([v_hi, v_lo]), last=np.stack([l_hi, l_lo]),
+        fa=np.concatenate([fa_hi, fa_lo], axis=1), plain=plain, full=full.astype(f), mix=mix.astype(f),
+        w2=np.stack([w_hi, w_lo]), v2=np.stack([v_hi, v_lo]), last=np.concatenate([l_hi, l_lo, l_hi], axis=1),
         tc=tc.astype(f), ts=ts.astype(f),
     )
 
@@ -101,7 +101,7 @@
 
 def dot_left(table, x):
     hi, lo = halves(x)
-    return dot(table[0], hi) + dot(table[0], lo) + dot(table[1], hi)
+    return dot(table[...], jnp.concatenate([hi, hi, lo], axis=0))
 
 
 def unpack_group(src, start, xs):
@@ -180,7 +180,7 @@
     def _(i):
         both = [xs[pl.ds(2 * i + q, SIDE, stride=GROUP), :] for q in range(2)]
         x = jnp.concatenate([jnp.where(v > LIMIT, 0.0, v) for v in both], axis=1).astype(BF)
-        res = dot(fa[0], x) + dot(fa[1], x)
+        res = dot(fa[...], jnp.concatenate([x, x], axis=0))
         z[2 * i] = res[:, :SIDE]
         z[2 * i + 1] = res[:, SIDE:]
 
@@ -218,7 +218,8 @@
 LANES = 512
 PARTS = NPIX // LANES
 TILES = NPIX // SIDE
-TURN = 37
+SLOTS = 4
+PER = LANES // SIDE
 
 
 def place():
@@ -226,14 +227,15 @@
     return wide, narrow, wide * 4 + narrow
 
 
-def partner(i):
+def partner(i, j):
     wide, narrow, _ = place()
-    s = i * TURN % NDEV
-    x = (wide // 8 + s % 4) % 4
-    y = (wide % 4 + s // 4 % 4) % 4
-    z = (wide // 4 % 2 * 2 + narrow // 2 + s // 16 % 4) % 4
-    core = (narrow % 2 + s // 64) % 2
-    return (x * 2 + z // 2) * 4 + y, z % 2 * 2 + core
+    x, y = lax.div(wide, 8), lax.rem(wide, 4)
+    z = lax.rem(lax.div(wide, 4), 2) * 2 + lax.div(narrow, 2)
+    x = lax.rem(x + i + j, 4)
+    y = lax.rem(y + i // 4 + j // 2 if isinstance(i, int) else y + lax.div(i, 4) + j // 2, 4)
+    z = lax.rem(z + j % 4, 4)
+    core = lax.rem(lax.rem(narrow, 2) + j // 4, 2)
+    return (x * 2 + lax.div(z, 2)) * 4 + y, lax.rem(z, 2) * 2 + core
 
 
 def columns(ref, row, device):
@@ -241,9 +243,8 @@
 
 
 def exchange(row, source, target, send_sem, recv_sem):
-    @pl.loop(1, NDEV)
-    def _(i):
-        wide, narrow = partner(i)
+    def send(i, j):
+        wide, narrow = partner(i, j)
         pltpu.make_async_remote_copy(
             src_ref=source(wide * 4 + narrow),
             dst_ref=target,
@@ -253,6 +254,14 @@
             device_id_type=pl.DeviceIdType.MESH,
         ).start()
 
+    @pl.loop(1, 16)
+    def _(i):
+        for j in range(8):
+            send(i, j)
+
+    for j in range(1, 8):
+        send(0, j)
+
 
 def wait_all(row, buffer, sem):
     block = buffer.at[row, pl.ds(0, NDEV - 1)]
@@ -264,25 +273,55 @@
     pltpu.make_async_copy(block, block, sem.at[row]).wait()
 
 
-def relayout_in(cube_v, work, part):
-    lanes = pl.ds(pl.multiple_of(part * LANES, LANES), LANES)
+def relayout_in(cube_v, slot, work, part):
     for c in range(0, SIDE, 16):
-        block = cube_v[pl.ds(c, 16), :, lanes].astype(F32).reshape(16 * ROWS, LANES)
-        for q in range(LANES // SIDE):
-            work[part * (LANES // SIDE) + q, pl.ds(c * ROWS, 16 * ROWS), :] = block[:, q * SIDE : (q + 1) * SIDE]
-
-
-def relayout_out(cube_v, work, part):
-    lanes = pl.ds(pl.multiple_of(part * LANES, LANES), LANES)
-    for c in range(0, SIDE, 16):
-        parts = [work[part * (LANES // SIDE) + q, pl.ds(c * ROWS, 16 * ROWS), :] for q in range(LANES // SIDE)]
-        cube_v[pl.ds(c, 16), :, lanes] = jnp.concatenate(parts, axis=1).reshape(16, ROWS, LANES).astype(BF)
+        block = cube_v[slot, pl.ds(c, 16), :, :].astype(F32).reshape(16 * ROWS, LANES)
+        for q in range(PER):
+            work[part * PER + q, pl.ds(c * ROWS, 16 * ROWS), :] = block[:, q * SIDE : (q + 1) * SIDE]
 
 
 def turn_in(row, tile, work, marks, sent):
     block = work[tile, pl.ds(row, SIDE, stride=ROWS), :]
-    turned = jnp.where(marks[...] > 0, FLAGGED, block.T)
+    turned = jnp.where(marks[0:1, :] > 0.0, FLAGGED, block.T)
     sent[row, pl.ds(pl.multiple_of(tile * SIDE, SIDE), SIDE), :] = turned.astype(BF)
+
+
+def make_marks(flags, marks):
+    lane = lax.broadcasted_iota(jnp.int32, (8, SIDE), 1)
+    value = jnp.zeros((8, SIDE), F32)
+    for f in range(SIDE // FLAGBLK):
+        inside = (lane >= f * FLAGBLK) & (lane < (f + 1) * FLAGBLK)
+        value = jnp.where(inside, flags[f].astype(F32), value)
+    marks[...] = value
+
+
+def make_taps(width, taps):
+    w = jnp.broadcast_to(width[...], (8, SIDE))
+    raw = [jnp.exp(-float((HALF - j) ** 2) / (2.0 * w * w)) for j in range(HALF + 1)]
+    total = raw[HALF]
+    for j in range(HALF):
+        total = total + 2.0 * raw[j]
+    for j in range(HALF + 1):
+        taps[j] = raw[j] / total
+
+
+def make_gain(line, gain):
+    half = SIDE // 2
+
+    def exact(a, b):
+        return jnp.dot(a, b, preferred_element_type=F32, precision=lax.Precision.HIGHEST)
+
+    low = line[...]
+    row = lax.broadcasted_iota(jnp.int32, (half, HROWS), 0)
+    col = lax.broadcasted_iota(jnp.int32, (half, HROWS), 1)
+    first = lax.broadcasted_iota(jnp.int32, (SIDE, SIDE), 0)
+    second = lax.broadcasted_iota(jnp.int32, (SIDE, SIDE), 1)
+    turned = exact(jnp.where(row + col == half - 1, 1.0, 0.0), low)
+    mirror = exact(turned, jnp.where(first + second == SIDE, 1.0, 0.0))
+    edge = exact(jnp.where(row + col == half, 1.0, 0.0), low)
+    lane = lax.broadcasted_iota(jnp.int32, (half, SIDE), 1)
+    high = jnp.where(lane == 0, edge, mirror)
+    gain[...] = jnp.concatenate([low[:half], high], axis=0).T[:HROWS] * (1.0 / NCHAN)
 
 
 def beam_start(row, back, padded):
@@ -308,19 +347,21 @@
 
 
 def strip_kernel(
-    cube, marks, gain, taps, fa, w2, v2, last, tc, ts, mix, full, plain, restored, continuum,
-    cube_v, work, sent, got, back, padded, flat, xs, z, tt, cs, fw, chol, shown, gathered,
+    cube, flags, line, width, fa, w2, v2, last, tc, ts, mix, full, plain, tiles, continuum,
+    cube_v, work, sent, got, back, padded, flat, leave, marks, taps, gain, xs, z, tt, cs, fw, chol, shown, gathered,
     in_sem, out_sem, go_send, go_recv, home_send, home_recv, own_sem, fit_send, fit_recv,
 ):
     my_wide, my_narrow, me = place()
 
     def cube_part(part):
         lanes = pl.ds(pl.multiple_of(part * LANES, LANES), LANES)
-        return pltpu.make_async_copy(cube.at[:, :, lanes], cube_v.at[:, :, lanes], in_sem.at[part])
+        slot = lax.rem(part, SLOTS)
+        return pltpu.make_async_copy(cube.at[:, :, lanes], cube_v.at[slot], in_sem.at[slot])
 
     def out_part(part):
-        lanes = pl.ds(pl.multiple_of(part * LANES, LANES), LANES)
-        return pltpu.make_async_copy(cube_v.at[:, :, lanes], restored.at[:, :, lanes], out_sem.at[part])
+        slot = lax.rem(part, 2)
+        target = tiles.at[pl.ds(part * PER, PER)]
+        return pltpu.make_async_copy(leave.at[slot], target, out_sem.at[slot])
 
     def own_go(row):
         return pltpu.make_async_copy(columns(sent, row, me), got.at[row, me], own_sem.at[row])
@@ -328,16 +369,23 @@
     def own_home(row):
         return pltpu.make_async_copy(got.at[row, me], columns(back, row, me), own_sem.at[ROWS + row])
 
-    @pl.loop(0, PARTS)
+    @pl.loop(0, SLOTS)
     def _(part):
         cube_part(part).start()
+
+    make_marks(flags, marks)
 
     @pl.loop(0, PARTS)
     def _(part):
         cube_part(part).wait()
-        relayout_in(cube_v, work, part)
-        for q in range(LANES // SIDE):
-            turn_in(0, part * (LANES // SIDE) + q, work, marks, sent)
+        relayout_in(cube_v, lax.rem(part, SLOTS), work, part)
+
+        @pl.when(part + SLOTS < PARTS)
+        def _():
+            cube_part(part + SLOTS).start()
+
+        for q in range(PER):
+            turn_in(0, part * PER + q, work, marks, sent)
 
     for row in range(ROWS):
         if row > 0:
@@ -348,6 +396,9 @@
 
         own_go(row).start()
         exchange(row, lambda d: columns(sent, row, d), got.at[row, me], go_send, go_recv)
+
+    make_gain(line, gain)
+    make_taps(width, taps)
 
     def fit_target(row):
         return row * (NDEV // ROWS) + me // ROWS
@@ -406,9 +457,15 @@
         else:
             @pl.loop(0, PARTS)
             def _(part):
-                for q in range(LANES // SIDE):
-                    beam_tile(row, part * (LANES // SIDE) + q, padded, taps, flat, work)
-                relayout_out(cube_v, work, part)
+                for q in range(PER):
+                    beam_tile(row, part * PER + q, padded, taps, flat, work)
+
+                @pl.when(part >= 2)
+                def _():
+                    out_part(part - 2).wait()
+
+                for q in range(PER):
+                    leave[lax.rem(part, 2), q] = work[part * PER + q].astype(BF)
                 out_part(part).start()
 
     for row in range(ROWS):
@@ -431,69 +488,65 @@
             pltpu.make_async_copy(block, block, fit_recv.at[slot]).wait()
 
     for slot in range(ROWS):
-        continuum[slot] = gathered[slot]
+        continuum[slot * OWN : (slot + 1) * OWN, :] = gathered[slot]
+    continuum[ROWS * OWN :, :] = jnp.zeros((2 * SIDE - ROWS * OWN, SIDE), F32)
     for row in range(ROWS):
         wait_rows(row, sent, go_send)
         wait_all(row, got, home_send)
 
-    @pl.loop(0, PARTS)
-    def _(part):
+    for part in (PARTS - 2, PARTS - 1):
         out_part(part).wait()
 
 
-def params():
-    return pltpu.CompilerParams(vmem_limit_bytes=VMEM_BYTES)
-
-
-def whole(array):
-    return pl.BlockSpec(array.shape, lambda *_: (0,) * array.ndim)
-
-
-def make_taps(widths):
-    offsets = jnp.arange(2 * HALF + 1, dtype=F32) - HALF
-    raw = jnp.exp(-offsets[:, None] ** 2 / (2.0 * widths[None, :] ** 2))
-    return raw / jnp.sum(raw, axis=0, keepdims=True)
-
-
-def gain_table(line_gain):
-    both = jnp.concatenate([line_gain, line_gain[1:-1][::-1]]) / NCHAN
-    return both.reshape(SIDE, SIDE).T[:HROWS]
+def leave_kernel(tiles, coefs, restored, continuum):
+    for c in range(0, SIDE, 16):
+        parts = [tiles[q, pl.ds(c * ROWS, 16 * ROWS), :].astype(F32) for q in range(PER)]
+        restored[pl.ds(c, 16), :, :] = jnp.concatenate(parts, axis=1).reshape(16, ROWS, LANES).astype(BF)
+    continuum[...] = coefs[...].T[:NBASIS, : ROWS * OWN]
+
+
+def params(**more):
+    return pltpu.CompilerParams(vmem_limit_bytes=VMEM_BYTES, **more)
 
 
 def body(cube, flags, line_gain, beam_width):
     tab = {k: jnp.asarray(v) for k, v in tables().items()}
-    gain = gain_table(line_gain)
-    taps = jnp.broadcast_to(make_taps(beam_width)[: HALF + 1, None, :], (HALF + 1, 8, SIDE))
-    marks = jnp.repeat(flags, FLAGBLK)[None, :]
+    line = jnp.pad(line_gain, (0, HROWS * SIDE - line_gain.shape[0])).reshape(HROWS, SIDE)
     names = ("fa", "w2", "v2", "last", "tc", "ts", "mix", "full", "plain")
-    ins = [marks, gain, taps] + [tab[n] for n in names]
+    ins = [line, beam_width[None, :]] + [tab[n] for n in names]
     dma = pltpu.SemaphoreType.DMA
-    restored, coefs = pl.pallas_call(
+    vmem = pltpu.VMEM
+    tiles, coefs = pl.pallas_call(
         strip_kernel,
-        in_specs=[pl.BlockSpec(memory_space=pl.ANY)] + [pl.BlockSpec(memory_space=pltpu.VMEM)] * len(ins),
-        out_specs=[pl.BlockSpec(memory_space=pl.ANY), pl.BlockSpec(memory_space=pltpu.VMEM)],
+        in_specs=[pl.BlockSpec(memory_space=pl.ANY), pl.BlockSpec(memory_space=pltpu.SMEM)]
+        + [pl.BlockSpec(memory_space=vmem)] * len(ins),
+        out_specs=[pl.BlockSpec(memory_space=pl.ANY), pl.BlockSpec(memory_space=vmem)],
         out_shape=[
-            jax.ShapeDtypeStruct((SIDE, ROWS, NPIX), BF),
-            jax.ShapeDtypeStruct((ROWS, OWN, SIDE), F32),
+            jax.ShapeDtypeStruct((TILES, SIDE * ROWS, SIDE), BF),
+            jax.ShapeDtypeStruct((2 * SIDE, SIDE), F32),
         ],
         scratch_shapes=[
-            pltpu.VMEM((SIDE, ROWS, NPIX), BF),
-            pltpu.VMEM((TILES, SIDE * ROWS, SIDE), F32),
-            pltpu.VMEM((ROWS, NPIX, SIDE), BF),
-            pltpu.VMEM((ROWS, NDEV, OWN, SIDE), BF),
-            pltpu.VMEM((ROWS, NPIX, SIDE), BF),
-            pltpu.VMEM((NPIX + 2 * HALF, SIDE), F32),
-            pltpu.VMEM((SIDE, SIDE), F32),
-            pltpu.VMEM((SIDE * GROUP, SIDE), F32),
-            pltpu.VMEM((GROUP, 2 * HROWS, SIDE), F32),
-            pltpu.VMEM((GROUP * 8, SIDE), F32),
-            pltpu.VMEM((NBASIS, GROUP, SIDE), F32),
-            pltpu.VMEM((NBASIS, 2 * HROWS, SIDE), F32),
-            pltpu.VMEM((NBASIS * NBASIS, 8, SIDE), F32),
-            pltpu.VMEM((ROWS, OWN, SIDE), F32),
-            pltpu.VMEM((ROWS, OWN, SIDE), F32),
-            dma((PARTS,)),
-            dma((PARTS,)),
+            vmem((SLOTS, SIDE, ROWS, LANES), BF),
+            vmem((TILES, SIDE * ROWS, SIDE), F32),
+            vmem((ROWS, NPIX, SIDE), BF),
+            vmem((ROWS, NDEV, OWN, SIDE), BF),
+            vmem((ROWS, NPIX, SIDE), BF),
+            vmem((NPIX + 2 * HALF, SIDE), F32),
+            vmem((SIDE, SIDE), F32),
+            vmem((2, PER, SIDE * ROWS, SIDE), BF),
+            vmem((8, SIDE), F32),
+            vmem((HALF + 1, 8, SIDE), F32),
+            vmem((HROWS, SIDE), F32),
+            vmem((SIDE * GROUP, SIDE), F32),
+            vmem((GROUP, 2 * HROWS, SIDE), F32),
+            vmem((GROUP * 8, SIDE), F32),
+            vmem((NBASIS, GROUP, SIDE), F32),
+            vmem((NBASIS, 2 * HROWS, SIDE), F32),
+            vmem((NBASIS * NBASIS, 8, SIDE), F32),
+            vmem((ROWS, OWN, SIDE), F32),
+            vmem((ROWS, OWN, SIDE), F32),
+            dma((SLOTS,)),
+            dma((2,)),
             dma((ROWS,)),
             dma((ROWS,)),
             dma((ROWS,)),
@@ -502,9 +555,25 @@
             dma((ROWS,)),
             dma((ROWS,)),
         ],
-        compiler_params=pltpu.CompilerParams(vmem_limit_bytes=VMEM_BYTES, has_side_effects=True),
-    )(cube, *ins)
-    continuum = coefs.reshape(ROWS * OWN, SIDE)[:, :NBASIS].T
+        compiler_params=params(has_side_effects=True),
+    )(cube, flags, *ins)
+    restored, continuum = pl.pallas_call(
+        leave_kernel,
+        grid=(PARTS,),
+        in_specs=[
+            pl.BlockSpec((PER, SIDE * ROWS, SIDE), lambda i: (i, 0, 0)),
+            pl.BlockSpec((2 * SIDE, SIDE), lambda i: (0, 0)),
+        ],
+        out_specs=[
+            pl.BlockSpec((SIDE, ROWS, LANES), lambda i: (0, 0, i)),
+            pl.BlockSpec((NBASIS, ROWS * OWN), lambda i: (0, 0)),
+        ],
+        out_shape=[
+            jax.ShapeDtypeStruct((SIDE, ROWS, NPIX), BF),
+            jax.ShapeDtypeStruct((NBASIS, ROWS * OWN), F32),
+        ],
+        compiler_params=params(),
+    )(tiles, coefs)
     return (restored, continuum)
 
 

time: 205 us -> 185 us (0.902); the launches traced: 205 us -> 182 us
  local copies, waits for them, and re-layouts: 13.7 us -> 1.39 us
  Pallas kernels: 189 us -> 180 us
    unnamed x4 -> x0, local copies, waits for them, and re-layouts: 10.2 us -> none
    pallas_call x1 -> x2, Pallas kernels: 189 us -> 180 us  [the longest x1 169 us: body(): pl.pallas_call(strip_kernel, in_specs=[pl.BlockSpec(memory_space=pl.ANY),...]
where the time goes in v2:
time: 185 us; the launch traced here: 182 us
  Pallas kernels  180 us (97%)
    pallas_call x1, Pallas kernels, body(): pl.pallas_call(strip_kernel, in_specs=[pl.BlockSpec(memory_space=pl.ANY),...  169 us
    pallas_call x1, Pallas kernels, body(): pl.pallas_call(leave_kernel, grid=(PARTS,), in_specs=[pl.BlockSpec((PER,...  10.2 us

profile of v2, /device:TPU:1, one launch (start us, length us, event | category | flops | bytes accessed | tf_op | source)
XLA Modules:
  0.0 181.8 jit_solution(9086657123113924756)
XLA Ops:
  0.6 1.4 pad_bitcast_fusion.line
  2.0 169.5 %shard_map.140 = (bf16[48,512,128]{2,1,0:T(8,128)(2,1)}, f32[256,128]{1,0:T(8,128)}) custom-call(bf16[128,4,6144]{2,1,0:T(4,128)(2,1)} %cube.1, s32[8]{0:T(128)} %flags.1, f32[72,128]{1,0:T(8,128)} %pad_bitcast_fusion.line, f32[1,128]{1,0:T(1,128)} %bitcast.3, bf16[144,256]{1,0:T(8,128)(2,1)} %constant.21.clone.fa, bf16[2,256,256]{2,1,0:T(8,128)(2,1)} %constant.25.clone.w2, ...), custom_call_target="tpu_custom_call" | custom-call | tf_op jit(solution)/shard_map/pallas_call | solution.py:519
  171.5 10.2 %shard_map.141 = (bf16[128,4,6144]{2,1,0:T(4,128)(2,1)}, f32[6,192]{1,0:T(8,128)}) custom-call(bf16[48,512,128]{2,1,0:T(8,128)(2,1)} %get-tuple-element.4.tiles, f32[256,128]{1,0:T(8,128)} %get-tuple-element.5.coefs), custom_call_target="tpu_custom_call" | custom-call | tf_op jit(solution)/shard_map/pallas_call | solution.py:560

commit v3 on v2

--- a/solution.py
+++ b/solution.py
@@ -20,6 +20,7 @@
 HROWS = 72
 OWN = NPIX // NDEV
 GROUP = 16
+STEP = GROUP + 1
 FLAGGED = 128.0
 LIMIT = 100.0
 BF = jnp.bfloat16
@@ -107,19 +108,21 @@
 def unpack_group(src, start, xs):
     @pl.loop(0, SIDE // 8)
     def _(i):
-        block = src[pl.ds(i * 8, 8), pl.ds(start, GROUP), :].astype(F32)
-        xs[pl.ds(pl.multiple_of(i * 8 * GROUP, 128), 8 * GROUP), :] = block.reshape(8 * GROUP, SIDE)
+        base = pl.multiple_of(i * 8 * STEP, 8)
+        for k in range(8):
+            xs[pl.ds(base + k * STEP, GROUP), :] = src[i * 8 + k, pl.ds(start, GROUP), :].astype(F32)
 
 
 def pack_group(dst, start, xs):
     @pl.loop(0, SIDE // 8)
     def _(i):
-        block = xs[pl.ds(pl.multiple_of(i * 8 * GROUP, 128), 8 * GROUP), :]
-        dst[pl.ds(i * 8, 8), pl.ds(start, GROUP), :] = block.reshape(8, GROUP, SIDE).astype(BF)
+        base = pl.multiple_of(i * 8 * STEP, 8)
+        for k in range(8):
+            dst[i * 8 + k, pl.ds(start, GROUP), :] = xs[pl.ds(base + k * STEP, GROUP), :].astype(BF)
 
 
 def fit_setup(xs, full, plain, fw, chol):
-    weight = jnp.where(xs[pl.ds(0, SIDE, stride=GROUP), :] > LIMIT, 0.0, 1.0)
+    weight = jnp.where(xs[pl.ds(0, SIDE, stride=STEP), :] > LIMIT, 0.0, 1.0)
     gram = {}
     for i in range(NBASIS):
         weighted = full[i] * weight
@@ -178,7 +181,7 @@
 def filter_group(xs, z, tt, cs, fa, w2, v2, last, tc, ts, gain, mix, fw, chol):
     @pl.loop(0, GROUP // 2)
     def _(i):
-        both = [xs[pl.ds(2 * i + q, SIDE, stride=GROUP), :] for q in range(2)]
+        both = [xs[pl.ds(2 * i + q, SIDE, stride=STEP), :] for q in range(2)]
         x = jnp.concatenate([jnp.where(v > LIMIT, 0.0, v) for v in both], axis=1).astype(BF)
         res = dot(fa[...], jnp.concatenate([x, x], axis=0))
         z[2 * i] = res[:, :SIDE]
@@ -210,16 +213,17 @@
             cols.append(jnp.concatenate([vr * tc[...] - vi * ts[...], vi * tc[...] + vr * ts[...]], axis=0))
         out = dot_left(last, jnp.concatenate(cols, axis=1))
         for q in range(quad):
-            xs[pl.ds(i * quad + q, SIDE, stride=GROUP), :] = out[:, q * SIDE : (q + 1) * SIDE]
+            xs[pl.ds(i * quad + q, SIDE, stride=STEP), :] = out[:, q * SIDE : (q + 1) * SIDE]
 
     return shown
 
 
-LANES = 512
-PARTS = NPIX // LANES
 TILES = NPIX // SIDE
+FLAT = TILES * ROWS
+REACH = FLAT + 1
+BLOCK = 8
+BLOCKS = SIDE // BLOCK
 SLOTS = 4
-PER = LANES // SIDE
 
 
 def place():
@@ -273,15 +277,20 @@
     pltpu.make_async_copy(block, block, sem.at[row]).wait()
 
 
-def relayout_in(cube_v, slot, work, part):
-    for c in range(0, SIDE, 16):
-        block = cube_v[slot, pl.ds(c, 16), :, :].astype(F32).reshape(16 * ROWS, LANES)
-        for q in range(PER):
-            work[part * PER + q, pl.ds(c * ROWS, 16 * ROWS), :] = block[:, q * SIDE : (q + 1) * SIDE]
+def widen(cube_v, slot, work, block):
+    base = pl.multiple_of(block * BLOCK * REACH, 8)
+    for k in range(BLOCK):
+        work[pl.ds(base + k * REACH, FLAT), :] = cube_v[slot, k].astype(F32)
+
+
+def narrow_down(leave, slot, work, block):
+    base = pl.multiple_of(block * BLOCK * REACH, 8)
+    for k in range(BLOCK):
+        leave[slot, k] = work[pl.ds(base + k * REACH, FLAT), :].astype(BF)
 
 
 def turn_in(row, tile, work, marks, sent):
-    block = work[tile, pl.ds(row, SIDE, stride=ROWS), :]
+    block = work[pl.ds(tile * ROWS + row, SIDE, stride=REACH), :]
     turned = jnp.where(marks[0:1, :] > 0.0, FLAGGED, block.T)
     sent[row, pl.ds(pl.multiple_of(tile * SIDE, SIDE), SIDE), :] = turned.astype(BF)
 
@@ -325,25 +334,31 @@
 
 
 def beam_start(row, back, padded):
-    padded[0:HALF, :] = jnp.zeros((HALF, SIDE), F32)
-    padded[HALF + NPIX : NPIX + 2 * HALF, :] = jnp.zeros((HALF, SIDE), F32)
+    last = (NPIX // GROUP + 1) * STEP
+    padded[0:GROUP, :] = jnp.zeros((GROUP, SIDE), F32)
+    padded[last : last + GROUP, :] = jnp.zeros((GROUP, SIDE), F32)
 
     @pl.loop(0, TILES)
     def _(i):
         at = pl.multiple_of(i * SIDE, SIDE)
-        padded[pl.ds(at + HALF, SIDE), :] = back[row, pl.ds(at, SIDE), :].astype(F32)
+        base = pl.multiple_of(i * 8 * STEP, 8)
+        for k in range(8):
+            padded[pl.ds(base + (k + 1) * STEP, GROUP), :] = back[row, pl.ds(at + k * GROUP, GROUP), :].astype(F32)
 
 
 def beam_tile(row, tile, padded, taps, flat, work):
-    at = tile * SIDE
-    run = SIDE // 8
-    values = [padded[pl.ds(at + t, 8, stride=run), :] for t in range(run + 2 * HALF)]
-    for t in range(run):
+    base = pl.multiple_of(tile * 8 * STEP, 8)
+    values = []
+    for t in range(-HALF, GROUP + HALF):
+        run, spot = t // GROUP, t % GROUP
+        values.append(padded[pl.ds(base + (run + 1) * STEP + spot, 8, stride=STEP), :])
+    for t in range(GROUP):
         total = values[t + HALF] * taps[HALF]
         for j in range(HALF):
             total = total + (values[t + j] + values[t + 2 * HALF - j]) * taps[j]
-        flat[pl.ds(t, 8, stride=run), :] = total
-    work[tile, pl.ds(row, SIDE, stride=ROWS), :] = flat[...].T
+        flat[pl.ds(t, 8, stride=STEP), :] = total
+    whole = jnp.concatenate([flat[k * STEP : k * STEP + GROUP, :] for k in range(8)], axis=0)
+    work[pl.ds(tile * ROWS + row, SIDE, stride=REACH), :] = whole.T
 
 
 def strip_kernel(
@@ -354,13 +369,13 @@
     my_wide, my_narrow, me = place()
 
     def cube_part(part):
-        lanes = pl.ds(pl.multiple_of(part * LANES, LANES), LANES)
         slot = lax.rem(part, SLOTS)
-        return pltpu.make_async_copy(cube.at[:, :, lanes], cube_v.at[slot], in_sem.at[slot])
+        source = cube.at[pl.ds(part * BLOCK, BLOCK)]
+        return pltpu.make_async_copy(source, cube_v.at[slot], in_sem.at[slot])
 
     def out_part(part):
         slot = lax.rem(part, 2)
-        target = tiles.at[pl.ds(part * PER, PER)]
+        target = tiles.at[pl.ds(part * BLOCK, BLOCK)]
         return pltpu.make_async_copy(leave.at[slot], target, out_sem.at[slot])
 
     def own_go(row):
@@ -375,24 +390,20 @@
 
     make_marks(flags, marks)
 
-    @pl.loop(0, PARTS)
+    @pl.loop(0, BLOCKS)
     def _(part):
         cube_part(part).wait()
-        relayout_in(cube_v, lax.rem(part, SLOTS), work, part)
-
-        @pl.when(part + SLOTS < PARTS)
+        widen(cube_v, lax.rem(part, SLOTS), work, part)
+
+        @pl.when(part + SLOTS < BLOCKS)
         def _():
             cube_part(part + SLOTS).start()
 
-        for q in range(PER):
-            turn_in(0, part * PER + q, work, marks, sent)
-
     for row in range(ROWS):
-        if row > 0:
-            @pl.loop(0, TILES, step=2)
-            def _(tile):
-                turn_in(row, tile, work, marks, sent)
-                turn_in(row, tile + 1, work, marks, sent)
+        @pl.loop(0, TILES, step=4)
+        def _(tile):
+            for q in range(4):
+                turn_in(row, tile + q, work, marks, sent)
 
         own_go(row).start()
         exchange(row, lambda d: columns(sent, row, d), got.at[row, me], go_send, go_recv)
@@ -450,23 +461,19 @@
         own_home(row).wait()
         wait_rows(row, back, home_recv)
         beam_start(row, back, padded)
-        if row < ROWS - 1:
-            @pl.loop(0, TILES)
-            def _(tile):
-                beam_tile(row, tile, padded, taps, flat, work)
-        else:
-            @pl.loop(0, PARTS)
-            def _(part):
-                for q in range(PER):
-                    beam_tile(row, part * PER + q, padded, taps, flat, work)
-
-                @pl.when(part >= 2)
-                def _():
-                    out_part(part - 2).wait()
-
-                for q in range(PER):
-                    leave[lax.rem(part, 2), q] = work[part * PER + q].astype(BF)
-                out_part(part).start()
+
+        @pl.loop(0, TILES)
+        def _(tile):
+            beam_tile(row, tile, padded, taps, flat, work)
+
+    @pl.loop(0, BLOCKS)
+    def _(part):
+        @pl.when(part >= 2)
+        def _():
+            out_part(part - 2).wait()
+
+        narrow_down(leave, lax.rem(part, 2), work, part)
+        out_part(part).start()
 
     for row in range(ROWS):
         dest = fit_target(row)
@@ -494,14 +501,12 @@
         wait_rows(row, sent, go_send)
         wait_all(row, got, home_send)
 
-    for part in (PARTS - 2, PARTS - 1):
+    for part in (BLOCKS - 2, BLOCKS - 1):
         out_part(part).wait()
 
 
 def leave_kernel(tiles, coefs, restored, continuum):
-    for c in range(0, SIDE, 16):
-        parts = [tiles[q, pl.ds(c * ROWS, 16 * ROWS), :].astype(F32) for q in range(PER)]
-        restored[pl.ds(c, 16), :, :] = jnp.concatenate(parts, axis=1).reshape(16, ROWS, LANES).astype(BF)
+    restored[...] = tiles[...]
     continuum[...] = coefs[...].T[:NBASIS, : ROWS * OWN]
 
 
@@ -516,28 +521,29 @@
     ins = [line, beam_width[None, :]] + [tab[n] for n in names]
     dma = pltpu.SemaphoreType.DMA
     vmem = pltpu.VMEM
+    flat = cube.reshape(SIDE, ROWS, TILES, SIDE).transpose(0, 2, 1, 3).reshape(SIDE, FLAT, SIDE)
     tiles, coefs = pl.pallas_call(
         strip_kernel,
         in_specs=[pl.BlockSpec(memory_space=pl.ANY), pl.BlockSpec(memory_space=pltpu.SMEM)]
         + [pl.BlockSpec(memory_space=vmem)] * len(ins),
         out_specs=[pl.BlockSpec(memory_space=pl.ANY), pl.BlockSpec(memory_space=vmem)],
         out_shape=[
-            jax.ShapeDtypeStruct((TILES, SIDE * ROWS, SIDE), BF),
+            jax.ShapeDtypeStruct((SIDE, FLAT, SIDE), BF),
             jax.ShapeDtypeStruct((2 * SIDE, SIDE), F32),
         ],
         scratch_shapes=[
-            vmem((SLOTS, SIDE, ROWS, LANES), BF),
-            vmem((TILES, SIDE * ROWS, SIDE), F32),
+            vmem((SLOTS, BLOCK, FLAT, SIDE), BF),
+            vmem((SIDE * REACH, SIDE), F32),
             vmem((ROWS, NPIX, SIDE), BF),
             vmem((ROWS, NDEV, OWN, SIDE), BF),
             vmem((ROWS, NPIX, SIDE), BF),
-            vmem((NPIX + 2 * HALF, SIDE), F32),
-            vmem((SIDE, SIDE), F32),
-            vmem((2, PER, SIDE * ROWS, SIDE), BF),
+            vmem(((NPIX // GROUP + 2) * STEP, SIDE), F32),
+            vmem((8 * STEP, SIDE), F32),
+            vmem((2, BLOCK, FLAT, SIDE), BF),
             vmem((8, SIDE), F32),
             vmem((HALF + 1, 8, SIDE), F32),
             vmem((HROWS, SIDE), F32),
-            vmem((SIDE * GROUP, SIDE), F32),
+            vmem((SIDE * STEP, SIDE), F32),
             vmem((GROUP, 2 * HROWS, SIDE), F32),
             vmem((GROUP * 8, SIDE), F32),
             vmem((NBASIS, GROUP, SIDE), F32),
@@ -556,24 +562,25 @@
             dma((ROWS,)),
         ],
         compiler_params=params(has_side_effects=True),
-    )(cube, flags, *ins)
+    )(flat, flags, *ins)
     restored, continuum = pl.pallas_call(
         leave_kernel,
-        grid=(PARTS,),
+        grid=(BLOCKS,),
         in_specs=[
-            pl.BlockSpec((PER, SIDE * ROWS, SIDE), lambda i: (i, 0, 0)),
+            pl.BlockSpec((BLOCK, FLAT, SIDE), lambda i: (i, 0, 0)),
             pl.BlockSpec((2 * SIDE, SIDE), lambda i: (0, 0)),
         ],
         out_specs=[
-            pl.BlockSpec((SIDE, ROWS, LANES), lambda i: (0, 0, i)),
+            pl.BlockSpec((BLOCK, FLAT, SIDE), lambda i: (i, 0, 0)),
             pl.BlockSpec((NBASIS, ROWS * OWN), lambda i: (0, 0)),
         ],
         out_shape=[
-            jax.ShapeDtypeStruct((SIDE, ROWS, NPIX), BF),
+            jax.ShapeDtypeStruct((SIDE, FLAT, SIDE), BF),
             jax.ShapeDtypeStruct((NBASIS, ROWS * OWN), F32),
         ],
         compiler_params=params(),
     )(tiles, coefs)
+    restored = restored.reshape(SIDE, TILES, ROWS, SIDE).transpose(0, 2, 1, 3).reshape(SIDE, ROWS, NPIX)
     return (restored, continuum)
 
 

time: 185 us -> 194 us (1.049)
  Pallas kernels: 180 us -> 190 us
    pallas_call x1, Pallas kernels: 169 us -> 179 us  [body(): pl.pallas_call(strip_kernel, in_specs=[pl.BlockSpec(memory_space=pl.ANY),...]
where the time goes in v3:
time: 194 us; the launch traced here: 192 us
  Pallas kernels  190 us (98%)
    pallas_call x1, Pallas kernels, body(): pl.pallas_call(strip_kernel, in_specs=[pl.BlockSpec(memory_space=pl.ANY),...  179 us
    pallas_call x1, Pallas kernels, body(): pl.pallas_call(leave_kernel, grid=(BLOCKS,), in_specs=[pl.BlockSpec((BLOC...  11 us

profile of v3, /device:TPU:1, one launch (start us, length us, event | category | flops | bytes accessed | tf_op | source)
XLA Modules:
  0.0 191.8 jit_solution(6502562320609689670)
XLA Ops:
  0.6 1.4 pad_bitcast_fusion.line
  2.0 178.8 %shard_map.140 = (bf16[128,192,128]{2,1,0:T(8,128)(2,1)}, f32[256,128]{1,0:T(8,128)}) custom-call(bf16[128,192,128]{2,1,0:T(8,128)(2,1)} %bitcast.13, s32[8]{0:T(128)} %flags.1, f32[72,128]{1,0:T(8,128)} %pad_bitcast_fusion.line, f32[1,128]{1,0:T(1,128)} %bitcast.14, bf16[144,256]{1,0:T(8,128)(2,1)} %constant.21.clone.fa, ...), custom_call_target="tpu_custom_call" | custom-call | tf_op jit(solution)/shard_map/pallas_call | solution.py:525
  180.8 11.0 %shard_map.141 = (bf16[128,192,128]{2,1,0:T(8,128)(2,1)}, f32[6,192]{1,0:T(8,128)}) custom-call(bf16[128,192,128]{2,1,0:T(8,128)(2,1)} %get-tuple-element.6.tiles, f32[256,128]{1,0:T(8,128)} %get-tuple-element.7.coefs), custom_call_target="tpu_custom_call" | custom-call | tf_op jit(solution)/shard_map/pallas_call | solution.py:566

commit v4 on v3

--- a/solution.py
+++ b/solution.py
@@ -20,7 +20,8 @@
 HROWS = 72
 OWN = NPIX // NDEV
 GROUP = 16
-STEP = GROUP + 1
+ZSTEP = 2 * HROWS + 8
+KEPT = SIDE // 2 + 1
 FLAGGED = 128.0
 LIMIT = 100.0
 BF = jnp.bfloat16
@@ -64,25 +65,22 @@
     fit = np.linalg.pinv(slow.T)
     mix = np.einsum("ma,kab->kmb", fit, full)
     mix = np.where(np.arange(NBASIS)[None, :, None] <= np.arange(NBASIS)[:, None, None], mix, 0.0)
-    w2 = np.block([[cos, -sin], [sin, cos]])
-    v2 = np.block([[cos, sin], [-sin, cos]])
     times = np.full((half,), 2.0)
     times[0] = times[-1] = 1.0
     last = np.zeros((SIDE, 2 * HROWS))
     last[:, :half] = cos[:, :half] * times
     last[:, HROWS : HROWS + half] = -sin[:, :half] * times
-    tc = np.zeros((HROWS, SIDE))
-    ts = np.zeros((HROWS, SIDE))
-    tc[:half] = np.cos(2.0 * np.pi / NCHAN * np.outer(idx[:half], idx))
-    ts[:half] = np.sin(2.0 * np.pi / NCHAN * np.outer(idx[:half], idx))
-    w_hi, w_lo, _ = split3(w2)
-    v_hi, v_lo, _ = split3(v2)
+    shift = np.arange(2 * SIDE) - SIDE
+    turn_c = np.zeros((HROWS, 2 * SIDE))
+    turn_s = np.zeros((HROWS, 2 * SIDE))
+    turn_c[:half] = np.cos(2.0 * np.pi / NCHAN * np.outer(idx[:half], shift))
+    turn_s[:half] = np.sin(2.0 * np.pi / NCHAN * np.outer(idx[:half], shift))
     l_hi, l_lo, _ = split3(last)
     f = np.float32
     return dict(
         fa=np.concatenate([fa_hi, fa_lo], axis=1), plain=plain, full=full.astype(f), mix=mix.astype(f),
-        w2=np.stack([w_hi, w_lo]), v2=np.stack([v_hi, v_lo]), last=np.concatenate([l_hi, l_lo, l_hi], axis=1),
-        tc=tc.astype(f), ts=ts.astype(f),
+        last=np.concatenate([l_hi, l_lo, l_hi], axis=1),
+        waves=np.stack([cos, sin]).astype(f), turns=np.stack([turn_c, turn_s]).astype(f),
     )
 
 
@@ -95,11 +93,6 @@
     return hi, (x - hi.astype(F32)).astype(BF)
 
 
-def dot_right(x, table):
-    hi, lo = halves(x)
-    return dot(hi, table[0]) + dot(lo, table[0]) + dot(hi, table[1])
-
-
 def dot_left(table, x):
     hi, lo = halves(x)
     return dot(table[...], jnp.concatenate([hi, hi, lo], axis=0))
@@ -108,25 +101,24 @@
 def unpack_group(src, start, xs):
     @pl.loop(0, SIDE // 8)
     def _(i):
-        base = pl.multiple_of(i * 8 * STEP, 8)
-        for k in range(8):
-            xs[pl.ds(base + k * STEP, GROUP), :] = src[i * 8 + k, pl.ds(start, GROUP), :].astype(F32)
+        block = src[pl.ds(i * 8, 8), pl.ds(start, GROUP), :].astype(F32)
+        xs[pl.ds(pl.multiple_of(i * 8 * GROUP, 128), 8 * GROUP), :] = block.reshape(8 * GROUP, SIDE)
 
 
 def pack_group(dst, start, xs):
     @pl.loop(0, SIDE // 8)
     def _(i):
-        base = pl.multiple_of(i * 8 * STEP, 8)
-        for k in range(8):
-            dst[i * 8 + k, pl.ds(start, GROUP), :] = xs[pl.ds(base + k * STEP, GROUP), :].astype(BF)
+        block = xs[pl.ds(pl.multiple_of(i * 8 * GROUP, 128), 8 * GROUP), :]
+        dst[pl.ds(i * 8, 8), pl.ds(start, GROUP), :] = block.reshape(8, GROUP, SIDE).astype(BF)
 
 
 def fit_setup(xs, full, plain, fw, chol):
-    weight = jnp.where(xs[pl.ds(0, SIDE, stride=STEP), :] > LIMIT, 0.0, 1.0)
+    weight = jnp.where(xs[pl.ds(0, SIDE, stride=GROUP), :] > LIMIT, 0.0, 1.0)
     gram = {}
+    fw[NBASIS * 2 * HROWS :, :] = jnp.zeros((2 * 2 * HROWS, SIDE), F32)
     for i in range(NBASIS):
         weighted = full[i] * weight
-        fw[i] = jnp.dot(plain[...], weighted, preferred_element_type=F32, precision=lax.Precision.HIGHEST)
+        fw[i * 2 * HROWS : (i + 1) * 2 * HROWS, :] = jnp.dot(plain[...], weighted, preferred_element_type=F32, precision=lax.Precision.HIGHEST)
         for j in range(i + 1):
             total = jnp.sum(jnp.sum(weighted * full[j], axis=0, keepdims=True), axis=1, keepdims=True)
             gram[i, j] = jnp.broadcast_to(total, (8, SIDE))
@@ -145,10 +137,33 @@
         chol[i * NBASIS + j] = value
 
 
-def fit_group(z, tt, mix, chol, cs):
+def make_matrices(gain, waves, turns, hs, mats):
+    def exact(a, b):
+        return jnp.dot(a, b, preferred_element_type=F32, precision=lax.Precision.HIGHEST)
+
+    real, imag = exact(gain[...], waves[0]), exact(gain[...], waves[1])
+    real, imag = jnp.concatenate([real, real], axis=1), jnp.concatenate([imag, imag], axis=1)
+    hs[0] = real * turns[0] - imag * turns[1]
+    hs[1] = real * turns[1] + imag * turns[0]
+
+    @pl.loop(0, KEPT)
+    def _(k):
+        for part in range(2):
+            rows = jnp.broadcast_to(hs[part, pl.ds(k, 1), :], (SIDE, 2 * SIDE))
+            matrix = pltpu.roll(rows, 0, 1, stride=1, stride_axis=0)[:, SIDE:]
+            hi, lo = halves(matrix)
+            mats[k, 2 * part] = hi
+            mats[k, 2 * part + 1] = lo
+            if part == 1:
+                mats[k, 4] = -hi
+                mats[k, 5] = -lo
+
+
+def fit_group(z, first, tt, mix, chol, cl):
     @pl.loop(0, GROUP)
     def _(p):
-        tt[pl.ds(pl.multiple_of(p * 8, 8), 8), :] = z[p, 64:72, :] + z[p, 136:144, :]
+        base = pl.multiple_of((first + p) * ZSTEP, 8)
+        tt[pl.ds(pl.multiple_of(p * 8, 8), 8), :] = z[pl.ds(base + 64, 8), :] + z[pl.ds(base + 136, 8), :]
 
     parts = [tt[pl.ds(m + 1, GROUP, stride=8), :] for m in range(NBASIS)]
 
@@ -172,58 +187,76 @@
         result[i] = value / entry(i, i)
     lane = lax.broadcasted_iota(jnp.int32, (GROUP, SIDE), 1)
     shown = jnp.zeros((GROUP, SIDE), F32)
+    parts = jnp.zeros((GROUP, SIDE), F32)
     for k in range(NBASIS):
-        cs[k] = result[k]
+        hi = result[k].astype(BF).astype(F32)
         shown = jnp.where(lane == k, result[k], shown)
+        parts = jnp.where((lane == k) | (lane == 16 + k), hi, parts)
+        parts = jnp.where(lane == 8 + k, result[k] - hi, parts)
+    cl[pl.ds(pl.multiple_of(first, GROUP), GROUP), :] = parts.astype(BF)
     return shown
 
 
-def filter_group(xs, z, tt, cs, fa, w2, v2, last, tc, ts, gain, mix, fw, chol):
-    @pl.loop(0, GROUP // 2)
+def spectrum_group(xs, z, first, fa):
+    @pl.loop(0, GROUP // 4)
     def _(i):
-        both = [xs[pl.ds(2 * i + q, SIDE, stride=STEP), :] for q in range(2)]
-        x = jnp.concatenate([jnp.where(v > LIMIT, 0.0, v) for v in both], axis=1).astype(BF)
-        res = dot(fa[...], jnp.concatenate([x, x], axis=0))
-        z[2 * i] = res[:, :SIDE]
-        z[2 * i + 1] = res[:, SIDE:]
-
-    shown = fit_group(z, tt, mix, chol, cs)
+        for h in range(2):
+            p = 4 * i + 2 * h
+            both = [xs[pl.ds(p + q, SIDE, stride=GROUP), :] for q in range(2)]
+            x = jnp.concatenate([jnp.where(v > LIMIT, 0.0, v) for v in both], axis=1).astype(BF)
+            res = dot(fa[...], jnp.concatenate([x, x], axis=0))
+            for q in range(2):
+                base = pl.multiple_of((first + p + q) * ZSTEP, 8)
+                z[pl.ds(base, 2 * HROWS), :] = res[:, q * SIDE : (q + 1) * SIDE]
+
+
+def filter_row(z, cl, fw, mats):
+    def one(k):
+        real, imag = pl.ds(k, OWN, stride=ZSTEP), pl.ds(k + HROWS, OWN, stride=ZSTEP)
+        base = jnp.concatenate(
+            [fw[pl.ds(k, 8, stride=2 * HROWS), :], fw[pl.ds(k + HROWS, 8, stride=2 * HROWS), :]], axis=1
+        )
+        hi = base.astype(BF).astype(F32)
+        fill = jnp.zeros((SIDE - 24, 2 * SIDE), F32)
+        smooth = dot(cl[...], jnp.concatenate([hi, hi, base - hi, fill], axis=0).astype(BF))
+        value = jnp.concatenate([z[real, :], z[imag, :]], axis=1) - smooth
+        hi, lo = halves(value)
+
+        def matrix(part):
+            up = jnp.concatenate([mats[k, part], mats[k, 2 + part]], axis=1)
+            down = jnp.concatenate([mats[k, 4 + part], mats[k, part]], axis=1)
+            return jnp.concatenate([up, down], axis=0)
+
+        both = dot(jnp.concatenate([hi, lo], axis=0), matrix(0))
+        out = both[:OWN] + both[OWN:] + dot(hi, matrix(1))
+        z[real, :] = out[:, :SIDE]
+        z[imag, :] = out[:, SIDE:]
+
+    @pl.loop(0, KEPT // 5)
+    def _(i):
+        for j in range(5):
+            one(i * 5 + j)
+
+
+def channels_group(xs, z, first, last):
     quad = 4
 
     @pl.loop(0, GROUP // quad)
     def _(i):
-        real, imag = [], []
-        for q in range(quad):
-            p = i * quad + q
-            zr, zi = z[p, :HROWS, :], z[p, HROWS:, :]
-            for k in range(NBASIS):
-                coef = cs[k, pl.ds(p, 1), :]
-                zr = zr - coef * fw[k, :HROWS, :]
-                zi = zi - coef * fw[k, HROWS:, :]
-            real.append(zr * tc[...] + zi * ts[...])
-            imag.append(zi * tc[...] - zr * ts[...])
-        u = jnp.concatenate([jnp.concatenate(real, axis=0), jnp.concatenate(imag, axis=0)], axis=1)
-        x = dot_right(u, w2)
-        g = jnp.concatenate([gain[...]] * quad, axis=0)
-        x = x * jnp.concatenate([g, g], axis=1)
-        v = dot_right(x, v2)
         cols = []
         for q in range(quad):
-            vr, vi = v[q * HROWS : (q + 1) * HROWS, :SIDE], v[q * HROWS : (q + 1) * HROWS, SIDE:]
-            cols.append(jnp.concatenate([vr * tc[...] - vi * ts[...], vi * tc[...] + vr * ts[...]], axis=0))
+            base = pl.multiple_of((first + i * quad + q) * ZSTEP, 8)
+            cols.append(z[pl.ds(base, 2 * HROWS), :])
         out = dot_left(last, jnp.concatenate(cols, axis=1))
         for q in range(quad):
-            xs[pl.ds(i * quad + q, SIDE, stride=STEP), :] = out[:, q * SIDE : (q + 1) * SIDE]
-
-    return shown
+            xs[pl.ds(i * quad + q, SIDE, stride=GROUP), :] = out[:, q * SIDE : (q + 1) * SIDE]
 
 
 TILES = NPIX // SIDE
 FLAT = TILES * ROWS
-REACH = FLAT + 1
+REACH = FLAT + 8
 BLOCK = 8
 BLOCKS = SIDE // BLOCK
-SLOTS = 4
 
 
 def place():
@@ -243,7 +276,7 @@
 
 
 def columns(ref, row, device):
-    return ref.at[row, pl.ds(pl.multiple_of(device * OWN, 16), OWN)]
+    return ref.at[pl.ds(pl.multiple_of(row * NPIX + device * OWN, 16), OWN)]
 
 
 def exchange(row, source, target, send_sem, recv_sem):
@@ -273,26 +306,28 @@
 
 
 def wait_rows(row, buffer, sem):
-    block = buffer.at[row, pl.ds(0, (NDEV - 1) * OWN)]
+    block = buffer.at[pl.ds(row * NPIX, (NDEV - 1) * OWN)]
     pltpu.make_async_copy(block, block, sem.at[row]).wait()
 
 
-def widen(cube_v, slot, work, block):
-    base = pl.multiple_of(block * BLOCK * REACH, 8)
+def widen(landing, work, block):
     for k in range(BLOCK):
-        work[pl.ds(base + k * REACH, FLAT), :] = cube_v[slot, k].astype(F32)
-
-
-def narrow_down(leave, slot, work, block):
-    base = pl.multiple_of(block * BLOCK * REACH, 8)
+        c = block * BLOCK + k
+        value = landing[pl.ds(pl.multiple_of(c * FLAT, 16), FLAT), :]
+        work[pl.ds(pl.multiple_of(c * REACH, 8), FLAT), :] = value.astype(F32)
+
+
+def narrow_down(leave, work, block):
     for k in range(BLOCK):
-        leave[slot, k] = work[pl.ds(base + k * REACH, FLAT), :].astype(BF)
+        c = block * BLOCK + k
+        value = work[pl.ds(pl.multiple_of(c * REACH, 8), FLAT), :]
+        leave[pl.ds(pl.multiple_of(c * FLAT, 16), FLAT), :] = value.astype(BF)
 
 
 def turn_in(row, tile, work, marks, sent):
     block = work[pl.ds(tile * ROWS + row, SIDE, stride=REACH), :]
     turned = jnp.where(marks[0:1, :] > 0.0, FLAGGED, block.T)
-    sent[row, pl.ds(pl.multiple_of(tile * SIDE, SIDE), SIDE), :] = turned.astype(BF)
+    sent[pl.ds(pl.multiple_of(row * NPIX + tile * SIDE, SIDE), SIDE), :] = turned.astype(BF)
 
 
 def make_marks(flags, marks):
@@ -334,49 +369,42 @@
 
 
 def beam_start(row, back, padded):
-    last = (NPIX // GROUP + 1) * STEP
-    padded[0:GROUP, :] = jnp.zeros((GROUP, SIDE), F32)
-    padded[last : last + GROUP, :] = jnp.zeros((GROUP, SIDE), F32)
+    padded[0:HALF, :] = jnp.zeros((HALF, SIDE), F32)
+    padded[HALF + NPIX : NPIX + 2 * HALF, :] = jnp.zeros((HALF, SIDE), F32)
 
     @pl.loop(0, TILES)
     def _(i):
         at = pl.multiple_of(i * SIDE, SIDE)
-        base = pl.multiple_of(i * 8 * STEP, 8)
-        for k in range(8):
-            padded[pl.ds(base + (k + 1) * STEP, GROUP), :] = back[row, pl.ds(at + k * GROUP, GROUP), :].astype(F32)
+        padded[pl.ds(at + HALF, SIDE), :] = back[pl.ds(pl.multiple_of(row * NPIX + at, SIDE), SIDE), :].astype(F32)
 
 
 def beam_tile(row, tile, padded, taps, flat, work):
-    base = pl.multiple_of(tile * 8 * STEP, 8)
-    values = []
-    for t in range(-HALF, GROUP + HALF):
-        run, spot = t // GROUP, t % GROUP
-        values.append(padded[pl.ds(base + (run + 1) * STEP + spot, 8, stride=STEP), :])
-    for t in range(GROUP):
+    at = tile * SIDE
+    run = SIDE // 8
+    values = [padded[pl.ds(at + t, 8, stride=run), :] for t in range(run + 2 * HALF)]
+    for t in range(run):
         total = values[t + HALF] * taps[HALF]
         for j in range(HALF):
             total = total + (values[t + j] + values[t + 2 * HALF - j]) * taps[j]
-        flat[pl.ds(t, 8, stride=STEP), :] = total
-    whole = jnp.concatenate([flat[k * STEP : k * STEP + GROUP, :] for k in range(8)], axis=0)
-    work[pl.ds(tile * ROWS + row, SIDE, stride=REACH), :] = whole.T
+        flat[pl.ds(t, 8, stride=run), :] = total
+    work[pl.ds(tile * ROWS + row, SIDE, stride=REACH), :] = flat[...].T
 
 
 def strip_kernel(
-    cube, flags, line, width, fa, w2, v2, last, tc, ts, mix, full, plain, tiles, continuum,
-    cube_v, work, sent, got, back, padded, flat, leave, marks, taps, gain, xs, z, tt, cs, fw, chol, shown, gathered,
+    cube, flags, line, width, fa, last, waves, turns, mix, full, plain, tiles, continuum,
+    work, sent, got, back, padded, flat, marks, taps, gain, hs, mats, xs, z, tt, cl, fw, chol, shown, gathered,
     in_sem, out_sem, go_send, go_recv, home_send, home_recv, own_sem, fit_send, fit_recv,
 ):
     my_wide, my_narrow, me = place()
 
+    def rows_of(part):
+        return pl.ds(pl.multiple_of(part * BLOCK * FLAT, 16), BLOCK * FLAT)
+
     def cube_part(part):
-        slot = lax.rem(part, SLOTS)
-        source = cube.at[pl.ds(part * BLOCK, BLOCK)]
-        return pltpu.make_async_copy(source, cube_v.at[slot], in_sem.at[slot])
+        return pltpu.make_async_copy(cube.at[rows_of(part)], back.at[rows_of(part)], in_sem.at[part])
 
     def out_part(part):
-        slot = lax.rem(part, 2)
-        target = tiles.at[pl.ds(part * BLOCK, BLOCK)]
-        return pltpu.make_async_copy(leave.at[slot], target, out_sem.at[slot])
+        return pltpu.make_async_copy(sent.at[rows_of(part)], tiles.at[rows_of(part)], out_sem.at[part])
 
     def own_go(row):
         return pltpu.make_async_copy(columns(sent, row, me), got.at[row, me], own_sem.at[row])
@@ -384,7 +412,7 @@
     def own_home(row):
         return pltpu.make_async_copy(got.at[row, me], columns(back, row, me), own_sem.at[ROWS + row])
 
-    @pl.loop(0, SLOTS)
+    @pl.loop(0, BLOCKS)
     def _(part):
         cube_part(part).start()
 
@@ -393,11 +421,7 @@
     @pl.loop(0, BLOCKS)
     def _(part):
         cube_part(part).wait()
-        widen(cube_v, lax.rem(part, SLOTS), work, part)
-
-        @pl.when(part + SLOTS < BLOCKS)
-        def _():
-            cube_part(part + SLOTS).start()
+        widen(back, work, part)
 
     for row in range(ROWS):
         @pl.loop(0, TILES, step=4)
@@ -410,6 +434,7 @@
 
     make_gain(line, gain)
     make_taps(width, taps)
+    make_matrices(gain, waves, turns, hs, mats)
 
     def fit_target(row):
         return row * (NDEV // ROWS) + me // ROWS
@@ -440,9 +465,15 @@
         def _(g):
             start = pl.multiple_of(g * GROUP, GROUP)
             unpack_group(rows, start, xs)
-            shown[row, pl.ds(start, GROUP), :] = filter_group(
-                xs, z, tt, cs, fa, w2, v2, last, tc, ts, gain, mix, fw, chol
-            )
+            spectrum_group(xs, z, start, fa)
+            shown[row, pl.ds(start, GROUP), :] = fit_group(z, start, tt, mix, chol, cl)
+
+        filter_row(z, cl, fw, mats)
+
+        @pl.loop(0, OWN // GROUP)
+        def _(g):
+            start = pl.multiple_of(g * GROUP, GROUP)
+            channels_group(xs, z, start, last)
             pack_group(rows, start, xs)
 
         own_home(row).start()
@@ -466,13 +497,12 @@
         def _(tile):
             beam_tile(row, tile, padded, taps, flat, work)
 
+    for row in range(ROWS):
+        wait_rows(row, sent, go_send)
+
     @pl.loop(0, BLOCKS)
     def _(part):
-        @pl.when(part >= 2)
-        def _():
-            out_part(part - 2).wait()
-
-        narrow_down(leave, lax.rem(part, 2), work, part)
+        narrow_down(sent, work, part)
         out_part(part).start()
 
     for row in range(ROWS):
@@ -498,16 +528,26 @@
         continuum[slot * OWN : (slot + 1) * OWN, :] = gathered[slot]
     continuum[ROWS * OWN :, :] = jnp.zeros((2 * SIDE - ROWS * OWN, SIDE), F32)
     for row in range(ROWS):
-        wait_rows(row, sent, go_send)
         wait_all(row, got, home_send)
 
-    for part in (BLOCKS - 2, BLOCKS - 1):
+    @pl.loop(0, BLOCKS)
+    def _(part):
         out_part(part).wait()
 
 
-def leave_kernel(tiles, coefs, restored, continuum):
-    restored[...] = tiles[...]
+def leave_kernel(tiles, coefs, restored, continuum, buffer, in_sem, out_sem):
+    def part(i, source, target, sem):
+        rows = pl.ds(pl.multiple_of(i * BLOCK * FLAT, 16), BLOCK * FLAT)
+        return pltpu.make_async_copy(source.at[rows], target.at[rows], sem.at[i])
+
+    for i in range(BLOCKS):
+        part(i, tiles, buffer, in_sem).start()
     continuum[...] = coefs[...].T[:NBASIS, : ROWS * OWN]
+    for i in range(BLOCKS):
+        part(i, tiles, buffer, in_sem).wait()
+        part(i, buffer, restored, out_sem).start()
+    for i in range(BLOCKS):
+        part(i, buffer, restored, out_sem).wait()
 
 
 def params(**more):
@@ -517,42 +557,42 @@
 def body(cube, flags, line_gain, beam_width):
     tab = {k: jnp.asarray(v) for k, v in tables().items()}
     line = jnp.pad(line_gain, (0, HROWS * SIDE - line_gain.shape[0])).reshape(HROWS, SIDE)
-    names = ("fa", "w2", "v2", "last", "tc", "ts", "mix", "full", "plain")
+    names = ("fa", "last", "waves", "turns", "mix", "full", "plain")
     ins = [line, beam_width[None, :]] + [tab[n] for n in names]
     dma = pltpu.SemaphoreType.DMA
     vmem = pltpu.VMEM
-    flat = cube.reshape(SIDE, ROWS, TILES, SIDE).transpose(0, 2, 1, 3).reshape(SIDE, FLAT, SIDE)
+    flat = cube.reshape(SIDE, ROWS, TILES, SIDE).transpose(0, 2, 1, 3).reshape(SIDE * FLAT, SIDE)
     tiles, coefs = pl.pallas_call(
         strip_kernel,
         in_specs=[pl.BlockSpec(memory_space=pl.ANY), pl.BlockSpec(memory_space=pltpu.SMEM)]
         + [pl.BlockSpec(memory_space=vmem)] * len(ins),
         out_specs=[pl.BlockSpec(memory_space=pl.ANY), pl.BlockSpec(memory_space=vmem)],
         out_shape=[
-            jax.ShapeDtypeStruct((SIDE, FLAT, SIDE), BF),
+            jax.ShapeDtypeStruct((SIDE * FLAT, SIDE), BF),
             jax.ShapeDtypeStruct((2 * SIDE, SIDE), F32),
         ],
         scratch_shapes=[
-            vmem((SLOTS, BLOCK, FLAT, SIDE), BF),
             vmem((SIDE * REACH, SIDE), F32),
-            vmem((ROWS, NPIX, SIDE), BF),
+            vmem((ROWS * NPIX, SIDE), BF),
             vmem((ROWS, NDEV, OWN, SIDE), BF),
-            vmem((ROWS, NPIX, SIDE), BF),
-            vmem(((NPIX // GROUP + 2) * STEP, SIDE), F32),
-            vmem((8 * STEP, SIDE), F32),
-            vmem((2, BLOCK, FLAT, SIDE), BF),
+            vmem((ROWS * NPIX, SIDE), BF),
+            vmem((NPIX + 2 * HALF, SIDE), F32),
+            vmem((SIDE, SIDE), F32),
             vmem((8, SIDE), F32),
             vmem((HALF + 1, 8, SIDE), F32),
             vmem((HROWS, SIDE), F32),
-            vmem((SIDE * STEP, SIDE), F32),
-            vmem((GROUP, 2 * HROWS, SIDE), F32),
+            vmem((2, HROWS, 2 * SIDE), F32),
+            vmem((KEPT, 6, SIDE, SIDE), BF),
+            vmem((SIDE * GROUP, SIDE), F32),
+            vmem((OWN * ZSTEP, SIDE), F32),
             vmem((GROUP * 8, SIDE), F32),
-            vmem((NBASIS, GROUP, SIDE), F32),
-            vmem((NBASIS, 2 * HROWS, SIDE), F32),
+            vmem((OWN, SIDE), BF),
+            vmem(((NBASIS + 2) * 2 * HROWS, SIDE), F32),
             vmem((NBASIS * NBASIS, 8, SIDE), F32),
             vmem((ROWS, OWN, SIDE), F32),
             vmem((ROWS, OWN, SIDE), F32),
-            dma((SLOTS,)),
-            dma((2,)),
+            dma((BLOCKS,)),
+            dma((BLOCKS,)),
             dma((ROWS,)),
             dma((ROWS,)),
             dma((ROWS,)),
@@ -565,19 +605,13 @@
     )(flat, flags, *ins)
     restored, continuum = pl.pallas_call(
         leave_kernel,
-        grid=(BLOCKS,),
-        in_specs=[
-            pl.BlockSpec((BLOCK, FLAT, SIDE), lambda i: (i, 0, 0)),
-            pl.BlockSpec((2 * SIDE, SIDE), lambda i: (0, 0)),
-        ],
-        out_specs=[
-            pl.BlockSpec((BLOCK, FLAT, SIDE), lambda i: (i, 0, 0)),
-            pl.BlockSpec((NBASIS, ROWS * OWN), lambda i: (0, 0)),
-        ],
+        in_specs=[pl.BlockSpec(memory_space=pl.ANY), pl.BlockSpec(memory_space=vmem)],
+        out_specs=[pl.BlockSpec(memory_space=pl.ANY), pl.BlockSpec(memory_space=vmem)],
         out_shape=[
-            jax.ShapeDtypeStruct((SIDE, FLAT, SIDE), BF),
+            jax.ShapeDtypeStruct((SIDE * FLAT, SIDE), BF),
             jax.ShapeDtypeStruct((NBASIS, ROWS * OWN), F32),
         ],
+        scratch_shapes=[vmem((SIDE * FLAT, SIDE), BF), dma((BLOCKS,)), dma((BLOCKS,))],
         compiler_params=params(),
     )(tiles, coefs)
     restored = restored.reshape(SIDE, TILES, ROWS, SIDE).transpose(0, 2, 1, 3).reshape(SIDE, ROWS, NPIX)

time: 194 us -> 186 us (0.959)
  Pallas kernels: 190 us -> 181 us
    pallas_call x1, Pallas kernels: 179 us -> 174 us  [body(): pl.pallas_call(strip_kernel, in_specs=[pl.BlockSpec(memory_space=pl.ANY),...]
    pallas_call x1, Pallas kernels: 11 us -> 6.98 us  [body(): pl.pallas_call(leave_kernel, in_specs=[pl.BlockSpec(memory_space=pl.ANY),...]
where the time goes in v4:
time: 186 us; the launch traced here: 183 us
  Pallas kernels  181 us (97%)
    pallas_call x1, Pallas kernels, body(): pl.pallas_call(strip_kernel, in_specs=[pl.BlockSpec(memory_space=pl.ANY),...  174 us
    pallas_call x1, Pallas kernels, body(): pl.pallas_call(leave_kernel, in_specs=[pl.BlockSpec(memory_space=pl.ANY),...  6.98 us

profile of v4, /device:TPU:1, one launch (start us, length us, event | category | flops | bytes accessed | tf_op | source)
XLA Modules:
  0.0 183.3 jit_solution(347502022282678899)
XLA Ops:
  0.6 1.4 pad_bitcast_fusion.line
  2.0 174.3 %shard_map.122 = (bf16[24576,128]{1,0:T(8,128)(2,1)}, f32[256,128]{1,0:T(8,128)}) custom-call(bf16[24576,128]{1,0:T(8,128)(2,1)} %bitcast.13, s32[8]{0:T(128)} %flags.1, f32[72,128]{1,0:T(8,128)} %pad_bitcast_fusion.line, f32[1,128]{1,0:T(1,128)} %bitcast.14, bf16[144,256]{1,0:T(8,128)(2,1)} %constant.17.clone.fa, bf16[128,432]{1,0:T(8,128)(2,1)} %constant.21.clone.last, ...), custom_call_target="tpu_custom_call" | custom-call | tf_op jit(solution)/shard_map/pallas_call | solution.py:565
  176.4 7.0 %shard_map.123 = (bf16[24576,128]{1,0:T(8,128)(2,1)}, f32[6,192]{1,0:T(8,128)}) custom-call(bf16[24576,128]{1,0:T(8,128)(2,1)} %get-tuple-element.6.tiles, f32[256,128]{1,0:T(8,128)} %get-tuple-element.7.coefs), custom_call_target="tpu_custom_call" | custom-call | tf_op jit(solution)/shard_map/pallas_call | solution.py:606

commit v5 on v4

--- a/solution.py
+++ b/solution.py
@@ -19,14 +19,14 @@
 SIDE = 128
 HROWS = 72
 OWN = NPIX // NDEV
-GROUP = 16
 ZSTEP = 2 * HROWS + 8
 KEPT = SIDE // 2 + 1
+BINS = 13
 FLAGGED = 128.0
 LIMIT = 100.0
 BF = jnp.bfloat16
 F32 = jnp.float32
-VMEM_BYTES = 56 * 1024 * 1024
+VMEM_BYTES = 61 * 1024 * 1024
 AXES = ("wide", "narrow")
 
 
@@ -98,22 +98,20 @@
     return dot(table[...], jnp.concatenate([hi, hi, lo], axis=0))
 
 
-def unpack_group(src, start, xs):
+def unpack_row(src, xs):
     @pl.loop(0, SIDE // 8)
     def _(i):
-        block = src[pl.ds(i * 8, 8), pl.ds(start, GROUP), :].astype(F32)
-        xs[pl.ds(pl.multiple_of(i * 8 * GROUP, 128), 8 * GROUP), :] = block.reshape(8 * GROUP, SIDE)
-
-
-def pack_group(dst, start, xs):
-    @pl.loop(0, SIDE // 8)
-    def _(i):
-        block = xs[pl.ds(pl.multiple_of(i * 8 * GROUP, 128), 8 * GROUP), :]
-        dst[pl.ds(i * 8, 8), pl.ds(start, GROUP), :] = block.reshape(8, GROUP, SIDE).astype(BF)
+        block = src[pl.ds(i * 8, 8), :, :].astype(F32)
+        xs[pl.ds(pl.multiple_of(i * 8 * OWN, 128), 8 * OWN), :] = block.reshape(8 * OWN, SIDE)
+
+
+def pack_block(dst, i, xs):
+    block = xs[pl.ds(pl.multiple_of(i * 8 * OWN, 128), 8 * OWN), :]
+    dst[pl.ds(i * 8, 8), :, :] = block.reshape(8, OWN, SIDE).astype(BF)
 
 
 def fit_setup(xs, full, plain, fw, chol):
-    weight = jnp.where(xs[pl.ds(0, SIDE, stride=GROUP), :] > LIMIT, 0.0, 1.0)
+    weight = jnp.where(xs[pl.ds(0, SIDE, stride=OWN), :] > LIMIT, 0.0, 1.0)
     gram = {}
     fw[NBASIS * 2 * HROWS :, :] = jnp.zeros((2 * 2 * HROWS, SIDE), F32)
     for i in range(NBASIS):
@@ -159,23 +157,21 @@
                 mats[k, 5] = -lo
 
 
-def fit_group(z, first, tt, mix, chol, cl):
-    @pl.loop(0, GROUP)
-    def _(p):
-        base = pl.multiple_of((first + p) * ZSTEP, 8)
-        tt[pl.ds(pl.multiple_of(p * 8, 8), 8), :] = z[pl.ds(base + 64, 8), :] + z[pl.ds(base + 136, 8), :]
-
-    parts = [tt[pl.ds(m + 1, GROUP, stride=8), :] for m in range(NBASIS)]
+def fit_row(z, mix, chol, cl):
+    parts = []
+    for m in range(NBASIS):
+        main = z[pl.ds(KEPT + m, OWN, stride=ZSTEP), :]
+        parts.append(main + z[pl.ds(HROWS + KEPT + m, OWN, stride=ZSTEP), :])
 
     def entry(i, j):
-        return jnp.broadcast_to(chol[i * NBASIS + j, 0:1, :], (GROUP, SIDE))
+        return jnp.broadcast_to(chol[i * NBASIS + j, 0:1, :], (OWN, SIDE))
 
     inner = []
     for k in range(NBASIS):
         total = parts[0] * mix[k, 0:1, :]
         for m in range(1, k + 1):
             total = total + parts[m] * mix[k, m : m + 1, :]
-        value = jnp.broadcast_to(jnp.sum(total, axis=1, keepdims=True), (GROUP, SIDE))
+        value = jnp.broadcast_to(jnp.sum(total, axis=1, keepdims=True), (OWN, SIDE))
         for j in range(k):
             value = value - entry(k, j) * inner[j]
         inner.append(value / entry(k, k))
@@ -185,42 +181,43 @@
         for j in range(i + 1, NBASIS):
             value = value - entry(j, i) * result[j]
         result[i] = value / entry(i, i)
-    lane = lax.broadcasted_iota(jnp.int32, (GROUP, SIDE), 1)
-    shown = jnp.zeros((GROUP, SIDE), F32)
-    parts = jnp.zeros((GROUP, SIDE), F32)
+    lane = lax.broadcasted_iota(jnp.int32, (OWN, SIDE), 1)
+    shown = jnp.zeros((OWN, SIDE), F32)
+    parts = jnp.zeros((OWN, SIDE), F32)
     for k in range(NBASIS):
         hi = result[k].astype(BF).astype(F32)
         shown = jnp.where(lane == k, result[k], shown)
         parts = jnp.where((lane == k) | (lane == 16 + k), hi, parts)
         parts = jnp.where(lane == 8 + k, result[k] - hi, parts)
-    cl[pl.ds(pl.multiple_of(first, GROUP), GROUP), :] = parts.astype(BF)
+    cl[...] = parts.astype(BF)
     return shown
 
 
-def spectrum_group(xs, z, first, fa):
-    @pl.loop(0, GROUP // 4)
+def spectrum_row(xs, z, fa):
+    @pl.loop(0, 8)
     def _(i):
-        for h in range(2):
-            p = 4 * i + 2 * h
-            both = [xs[pl.ds(p + q, SIDE, stride=GROUP), :] for q in range(2)]
+        for h in range(3):
+            p = 6 * i + 2 * h
+            both = [xs[pl.ds(p + q, SIDE, stride=OWN), :] for q in range(2)]
             x = jnp.concatenate([jnp.where(v > LIMIT, 0.0, v) for v in both], axis=1).astype(BF)
             res = dot(fa[...], jnp.concatenate([x, x], axis=0))
             for q in range(2):
-                base = pl.multiple_of((first + p + q) * ZSTEP, 8)
+                base = pl.multiple_of((p + q) * ZSTEP, 8)
                 z[pl.ds(base, 2 * HROWS), :] = res[:, q * SIDE : (q + 1) * SIDE]
 
 
 def filter_row(z, cl, fw, mats):
-    def one(k):
-        real, imag = pl.ds(k, OWN, stride=ZSTEP), pl.ds(k + HROWS, OWN, stride=ZSTEP)
+    def rows(k):
+        return pl.ds(k, OWN, stride=ZSTEP), pl.ds(k + HROWS, OWN, stride=ZSTEP)
+
+    def one(k, value):
         base = jnp.concatenate(
             [fw[pl.ds(k, 8, stride=2 * HROWS), :], fw[pl.ds(k + HROWS, 8, stride=2 * HROWS), :]], axis=1
         )
         hi = base.astype(BF).astype(F32)
         fill = jnp.zeros((SIDE - 24, 2 * SIDE), F32)
         smooth = dot(cl[...], jnp.concatenate([hi, hi, base - hi, fill], axis=0).astype(BF))
-        value = jnp.concatenate([z[real, :], z[imag, :]], axis=1) - smooth
-        hi, lo = halves(value)
+        hi, lo = halves(value - smooth)
 
         def matrix(part):
             up = jnp.concatenate([mats[k, part], mats[k, 2 + part]], axis=1)
@@ -228,28 +225,35 @@
             return jnp.concatenate([up, down], axis=0)
 
         both = dot(jnp.concatenate([hi, lo], axis=0), matrix(0))
-        out = both[:OWN] + both[OWN:] + dot(hi, matrix(1))
-        z[real, :] = out[:, :SIDE]
-        z[imag, :] = out[:, SIDE:]
-
-    @pl.loop(0, KEPT // 5)
+        return both[:OWN] + both[OWN:] + dot(hi, matrix(1))
+
+    @pl.loop(0, KEPT // BINS)
     def _(i):
-        for j in range(5):
-            one(i * 5 + j)
-
-
-def channels_group(xs, z, first, last):
+        values = []
+        for j in range(BINS):
+            real, imag = rows(i * BINS + j)
+            values.append(jnp.concatenate([z[real, :], z[imag, :]], axis=1))
+        values = [one(i * BINS + j, value) for j, value in enumerate(values)]
+        for j, value in enumerate(values):
+            real, imag = rows(i * BINS + j)
+            z[real, :] = value[:, :SIDE]
+            z[imag, :] = value[:, SIDE:]
+
+
+def channels_row(xs, z, last):
     quad = 4
 
-    @pl.loop(0, GROUP // quad)
+    @pl.loop(0, OWN // (2 * quad))
     def _(i):
-        cols = []
-        for q in range(quad):
-            base = pl.multiple_of((first + i * quad + q) * ZSTEP, 8)
-            cols.append(z[pl.ds(base, 2 * HROWS), :])
-        out = dot_left(last, jnp.concatenate(cols, axis=1))
-        for q in range(quad):
-            xs[pl.ds(i * quad + q, SIDE, stride=GROUP), :] = out[:, q * SIDE : (q + 1) * SIDE]
+        for h in range(2):
+            first = (2 * i + h) * quad
+            cols = []
+            for q in range(quad):
+                base = pl.multiple_of((first + q) * ZSTEP, 8)
+                cols.append(z[pl.ds(base, 2 * HROWS), :])
+            out = dot_left(last, jnp.concatenate(cols, axis=1))
+            for q in range(quad):
+                xs[pl.ds(first + q, SIDE, stride=OWN), :] = out[:, q * SIDE : (q + 1) * SIDE]
 
 
 TILES = NPIX // SIDE
@@ -264,40 +268,40 @@
     return wide, narrow, wide * 4 + narrow
 
 
-def partner(i, j):
-    wide, narrow, _ = place()
-    x, y = lax.div(wide, 8), lax.rem(wide, 4)
-    z = lax.rem(lax.div(wide, 4), 2) * 2 + lax.div(narrow, 2)
-    x = lax.rem(x + i + j, 4)
-    y = lax.rem(y + i // 4 + j // 2 if isinstance(i, int) else y + lax.div(i, 4) + j // 2, 4)
-    z = lax.rem(z + j % 4, 4)
-    core = lax.rem(lax.rem(narrow, 2) + j // 4, 2)
-    return (x * 2 + lax.div(z, 2)) * 4 + y, lax.rem(z, 2) * 2 + core
-
-
 def columns(ref, row, device):
     return ref.at[pl.ds(pl.multiple_of(row * NPIX + device * OWN, 16), OWN)]
 
 
-def exchange(row, source, target, send_sem, recv_sem):
+def exchange(row, make, source, target, send_sem, recv_sem):
+    _, _, me = place()
+
+    def block_of(i):
+        return lax.rem(lax.div(me, 8) + 5 * i, 16)
+
     def send(i, j):
-        wide, narrow = partner(i, j)
+        device = block_of(i) * 8 + lax.rem(lax.rem(me, 8) + j, 8)
         pltpu.make_async_remote_copy(
-            src_ref=source(wide * 4 + narrow),
+            src_ref=source(device),
             dst_ref=target,
             send_sem=send_sem.at[row],
             recv_sem=recv_sem.at[row],
-            device_id=(wide, narrow),
+            device_id=(lax.div(device, 4), lax.rem(device, 4)),
             device_id_type=pl.DeviceIdType.MESH,
         ).start()
 
-    @pl.loop(1, 16)
+    make(block_of(0))
+    for j in range(1, 8):
+        send(0, j)
+    make(block_of(1))
+
+    @pl.loop(2, 16)
     def _(i):
         for j in range(8):
-            send(i, j)
-
-    for j in range(1, 8):
-        send(0, j)
+            send(i - 1, j)
+        make(block_of(i))
+
+    for j in range(8):
+        send(15, j)
 
 
 def wait_all(row, buffer, sem):
@@ -387,12 +391,21 @@
         for j in range(HALF):
             total = total + (values[t + j] + values[t + 2 * HALF - j]) * taps[j]
         flat[pl.ds(t, 8, stride=run), :] = total
-    work[pl.ds(tile * ROWS + row, SIDE, stride=REACH), :] = flat[...].T
+
+
+def beam_row(row, padded, taps, flats, work):
+    @pl.loop(0, TILES // len(flats))
+    def _(i):
+        for q, flat in enumerate(flats):
+            beam_tile(row, i * len(flats) + q, padded, taps, flat, work)
+        for q, flat in enumerate(flats):
+            tile = i * len(flats) + q
+            work[pl.ds(tile * ROWS + row, SIDE, stride=REACH), :] = flat[...].T
 
 
 def strip_kernel(
     cube, flags, line, width, fa, last, waves, turns, mix, full, plain, tiles, continuum,
-    work, sent, got, back, padded, flat, marks, taps, gain, hs, mats, xs, z, tt, cl, fw, chol, shown, gathered,
+    work, sent, got, back, padded, flat0, flat1, flat2, flat3, marks, taps, gain, hs, mats, xs, z, cl, fw, chol, shown, gathered,
     in_sem, out_sem, go_send, go_recv, home_send, home_recv, own_sem, fit_send, fit_recv,
 ):
     my_wide, my_narrow, me = place()
@@ -424,13 +437,12 @@
         widen(back, work, part)
 
     for row in range(ROWS):
-        @pl.loop(0, TILES, step=4)
-        def _(tile):
-            for q in range(4):
-                turn_in(row, tile + q, work, marks, sent)
-
+        def make(block):
+            for q in range(3):
+                turn_in(row, block * 3 + q, work, marks, sent)
+
+        exchange(row, make, lambda d: columns(sent, row, d), got.at[row, me], go_send, go_recv)
         own_go(row).start()
-        exchange(row, lambda d: columns(sent, row, d), got.at[row, me], go_send, go_recv)
 
     make_gain(line, gain)
     make_taps(width, taps)
@@ -457,27 +469,17 @@
         own_go(row).wait()
         wait_all(row, got, go_recv)
         rows = got.at[row]
+        unpack_row(rows, xs)
         if row == 0:
-            unpack_group(rows, 0, xs)
             fit_setup(xs, full, plain, fw, chol)
-
-        @pl.loop(0, OWN // GROUP)
-        def _(g):
-            start = pl.multiple_of(g * GROUP, GROUP)
-            unpack_group(rows, start, xs)
-            spectrum_group(xs, z, start, fa)
-            shown[row, pl.ds(start, GROUP), :] = fit_group(z, start, tt, mix, chol, cl)
-
+        spectrum_row(xs, z, fa)
+        shown[row] = fit_row(z, mix, chol, cl)
         filter_row(z, cl, fw, mats)
-
-        @pl.loop(0, OWN // GROUP)
-        def _(g):
-            start = pl.multiple_of(g * GROUP, GROUP)
-            channels_group(xs, z, start, last)
-            pack_group(rows, start, xs)
-
+        channels_row(xs, z, last)
+        exchange(
+            row, lambda i: pack_block(rows, i, xs), lambda d: got.at[row, d], columns(back, row, me), home_send, home_recv
+        )
         own_home(row).start()
-        exchange(row, lambda d: got.at[row, d], columns(back, row, me), home_send, home_recv)
         dest = fit_target(row)
 
         @pl.when(dest != me)
@@ -492,10 +494,7 @@
         own_home(row).wait()
         wait_rows(row, back, home_recv)
         beam_start(row, back, padded)
-
-        @pl.loop(0, TILES)
-        def _(tile):
-            beam_tile(row, tile, padded, taps, flat, work)
+        beam_row(row, padded, taps, (flat0, flat1, flat2, flat3), work)
 
     for row in range(ROWS):
         wait_rows(row, sent, go_send)
@@ -578,14 +577,16 @@
             vmem((ROWS * NPIX, SIDE), BF),
             vmem((NPIX + 2 * HALF, SIDE), F32),
             vmem((SIDE, SIDE), F32),
+            vmem((SIDE, SIDE), F32),
+            vmem((SIDE, SIDE), F32),
+            vmem((SIDE, SIDE), F32),
             vmem((8, SIDE), F32),
             vmem((HALF + 1, 8, SIDE), F32),
             vmem((HROWS, SIDE), F32),
             vmem((2, HROWS, 2 * SIDE), F32),
             vmem((KEPT, 6, SIDE, SIDE), BF),
-            vmem((SIDE * GROUP, SIDE), F32),
+            vmem((SIDE * OWN, SIDE), F32),
             vmem((OWN * ZSTEP, SIDE), F32),
-            vmem((GROUP * 8, SIDE), F32),
             vmem((OWN, SIDE), BF),
             vmem(((NBASIS + 2) * 2 * HROWS, SIDE), F32),
             vmem((NBASIS * NBASIS, 8, SIDE), F32),

time: 186 us -> 213 us (1.15)
  the two profiles are of different devices: /device:TPU:1 before, /device:TPU:4 now
where the time goes in v5:
time: 213 us; the launch traced here: 212 us
  Pallas kernels  210 us (99%)
    pallas_call x1, Pallas kernels, body(): pl.pallas_call(strip_kernel, in_specs=[pl.BlockSpec(memory_space=pl.ANY),...  203 us
    pallas_call x1, Pallas kernels, body(): pl.pallas_call(leave_kernel, in_specs=[pl.BlockSpec(memory_space=pl.ANY),...  6.98 us

profile of v5, /device:TPU:4, one launch (start us, length us, event | category | flops | bytes accessed | tf_op | source)
XLA Modules:
  0.0 212.3 jit_solution(14171729976771274720)
XLA Ops:
  0.6 1.4 pad_bitcast_fusion.line
  2.0 203.3 %shard_map.122 = (bf16[24576,128]{1,0:T(8,128)(2,1)}, f32[256,128]{1,0:T(8,128)}) custom-call(bf16[24576,128]{1,0:T(8,128)(2,1)} %bitcast.13, s32[8]{0:T(128)} %flags.1, f32[72,128]{1,0:T(8,128)} %pad_bitcast_fusion.line, f32[1,128]{1,0:T(1,128)} %bitcast.14, bf16[144,256]{1,0:T(8,128)(2,1)} %constant.17.clone.fa, bf16[128,432]{1,0:T(8,128)(2,1)} %constant.21.clone.last, ...), custom_call_target="tpu_custom_call" | custom-call | tf_op jit(solution)/shard_map/pallas_call | solution.py:564
  205.3 7.0 %shard_map.123 = (bf16[24576,128]{1,0:T(8,128)(2,1)}, f32[6,192]{1,0:T(8,128)}) custom-call(bf16[24576,128]{1,0:T(8,128)(2,1)} %get-tuple-element.6.tiles, f32[256,128]{1,0:T(8,128)} %get-tuple-element.7.coefs), custom_call_target="tpu_custom_call" | custom-call | tf_op jit(solution)/shard_map/pallas_call | solution.py:607

commit v6 on v5

--- a/solution.py
+++ b/solution.py
@@ -259,6 +259,8 @@
 TILES = NPIX // SIDE
 FLAT = TILES * ROWS
 REACH = FLAT + 8
+PART = 4 * ROWS
+PARTS = FLAT // PART
 BLOCK = 8
 BLOCKS = SIDE // BLOCK
 
@@ -269,39 +271,44 @@
 
 
 def columns(ref, row, device):
-    return ref.at[pl.ds(pl.multiple_of(row * NPIX + device * OWN, 16), OWN)]
-
-
-def exchange(row, make, source, target, send_sem, recv_sem):
-    _, _, me = place()
-
-    def block_of(i):
-        return lax.rem(lax.div(me, 8) + 5 * i, 16)
-
+    slab = row * (NPIX // FLAT) + lax.div(device, 4)
+    return ref.at[slab, pl.ds(pl.multiple_of(lax.rem(device, 4) * OWN, 16), OWN)]
+
+
+def partner(i, j):
+    wide, narrow, _ = place()
+    x, y = lax.div(wide, 8), lax.rem(wide, 4)
+    z = lax.rem(lax.div(wide, 4), 2) * 2 + lax.div(narrow, 2)
+    x = lax.rem(x + i + j, 4)
+    y = lax.rem(y + (i // 4 if isinstance(i, int) else lax.div(i, 4)) + j // 2, 4)
+    z = lax.rem(z + j % 4, 4)
+    core = lax.rem(lax.rem(narrow, 2) + j // 4, 2)
+    return (x * 2 + lax.div(z, 2)) * 4 + y, lax.rem(z, 2) * 2 + core
+
+
+def exchange(row, source, target, send_sem, recv_sem, beside=None):
     def send(i, j):
-        device = block_of(i) * 8 + lax.rem(lax.rem(me, 8) + j, 8)
+        wide, narrow = partner(i, j)
         pltpu.make_async_remote_copy(
-            src_ref=source(device),
+            src_ref=source(wide * 4 + narrow),
             dst_ref=target,
             send_sem=send_sem.at[row],
             recv_sem=recv_sem.at[row],
-            device_id=(lax.div(device, 4), lax.rem(device, 4)),
+            device_id=(wide, narrow),
             device_id_type=pl.DeviceIdType.MESH,
         ).start()
 
-    make(block_of(0))
+    @pl.loop(1, 16)
+    def _(i):
+        for j in range(8):
+            send(i, j)
+        if beside is not None:
+            beside(i)
+
     for j in range(1, 8):
         send(0, j)
-    make(block_of(1))
-
-    @pl.loop(2, 16)
-    def _(i):
-        for j in range(8):
-            send(i - 1, j)
-        make(block_of(i))
-
-    for j in range(8):
-        send(15, j)
+    if beside is not None:
+        beside(0)
 
 
 def wait_all(row, buffer, sem):
@@ -309,29 +316,34 @@
     pltpu.make_async_copy(block, block, sem.at[row]).wait()
 
 
-def wait_rows(row, buffer, sem):
-    block = buffer.at[pl.ds(row * NPIX, (NDEV - 1) * OWN)]
-    pltpu.make_async_copy(block, block, sem.at[row]).wait()
-
-
-def widen(landing, work, block):
-    for k in range(BLOCK):
-        c = block * BLOCK + k
-        value = landing[pl.ds(pl.multiple_of(c * FLAT, 16), FLAT), :]
-        work[pl.ds(pl.multiple_of(c * REACH, 8), FLAT), :] = value.astype(F32)
+def part_rows(part):
+    return pl.ds(pl.multiple_of(part * PART, 16), PART)
+
+
+def widen(landing, work, part):
+    @pl.loop(0, SIDE // 8)
+    def _(i):
+        for k in range(8):
+            c = i * 8 + k
+            value = landing[c, part_rows(part), :]
+            work[pl.ds(pl.multiple_of(c * REACH + part * PART, 8), PART), :] = value.astype(F32)
 
 
 def narrow_down(leave, work, block):
     for k in range(BLOCK):
         c = block * BLOCK + k
         value = work[pl.ds(pl.multiple_of(c * REACH, 8), FLAT), :]
-        leave[pl.ds(pl.multiple_of(c * FLAT, 16), FLAT), :] = value.astype(BF)
+        leave[c] = value.astype(BF)
 
 
 def turn_in(row, tile, work, marks, sent):
     block = work[pl.ds(tile * ROWS + row, SIDE, stride=REACH), :]
-    turned = jnp.where(marks[0:1, :] > 0.0, FLAGGED, block.T)
-    sent[pl.ds(pl.multiple_of(row * NPIX + tile * SIDE, SIDE), SIDE), :] = turned.astype(BF)
+    turned = jnp.where(marks[0:1, :] > 0.0, FLAGGED, block.T).astype(BF)
+    for h in range(2):
+        place_at = tile * 2 + h
+        slab = row * (NPIX // FLAT) + lax.div(place_at, 3)
+        start = pl.multiple_of(lax.rem(place_at, 3) * (SIDE // 2), 16)
+        sent[slab, pl.ds(start, SIDE // 2), :] = turned[h * (SIDE // 2) : (h + 1) * (SIDE // 2)]
 
 
 def make_marks(flags, marks):
@@ -359,7 +371,8 @@
     def exact(a, b):
         return jnp.dot(a, b, preferred_element_type=F32, precision=lax.Precision.HIGHEST)
 
-    low = line[...]
+    low = jnp.concatenate([line[pl.ds(k * SIDE, SIDE)].reshape(1, SIDE) for k in range(half)], axis=0)
+    low = jnp.concatenate([low, jnp.broadcast_to(line[pl.ds(half * SIDE, 1)].reshape(1, 1), (8, SIDE))], axis=0)
     row = lax.broadcasted_iota(jnp.int32, (half, HROWS), 0)
     col = lax.broadcasted_iota(jnp.int32, (half, HROWS), 1)
     first = lax.broadcasted_iota(jnp.int32, (SIDE, SIDE), 0)
@@ -376,10 +389,10 @@
     padded[0:HALF, :] = jnp.zeros((HALF, SIDE), F32)
     padded[HALF + NPIX : NPIX + 2 * HALF, :] = jnp.zeros((HALF, SIDE), F32)
 
-    @pl.loop(0, TILES)
+    @pl.loop(0, NPIX // FLAT)
     def _(i):
-        at = pl.multiple_of(i * SIDE, SIDE)
-        padded[pl.ds(at + HALF, SIDE), :] = back[pl.ds(pl.multiple_of(row * NPIX + at, SIDE), SIDE), :].astype(F32)
+        at = pl.multiple_of(i * FLAT + HALF, 8)
+        padded[pl.ds(at, FLAT), :] = back[row * (NPIX // FLAT) + i].astype(F32)
 
 
 def beam_tile(row, tile, padded, taps, flat, work):
@@ -404,46 +417,60 @@
 
 
 def strip_kernel(
-    cube, flags, line, width, fa, last, waves, turns, mix, full, plain, tiles, continuum,
-    work, sent, got, back, padded, flat0, flat1, flat2, flat3, marks, taps, gain, hs, mats, xs, z, cl, fw, chol, shown, gathered,
-    in_sem, out_sem, go_send, go_recv, home_send, home_recv, own_sem, fit_send, fit_recv,
+    cube, flags, line, width, fa_in, last_in, waves_in, turns_in, mix_in, full_in, plain_in, tiles, final, continuum,
+    work, sent, got, back, padded, flat0, flat1, flat2, flat3, marks, taps, gain, hs, mats, xs, z, cl, fw, chol,
+    shown, gathered, fa, last, waves, turns, mix, full, plain,
+    in_sem, out_sem, table_sem, go_send, go_recv, home_send, home_recv, own_sem, fit_send, fit_recv,
 ):
     my_wide, my_narrow, me = place()
-
-    def rows_of(part):
-        return pl.ds(pl.multiple_of(part * BLOCK * FLAT, 16), BLOCK * FLAT)
+    tables_in = (fa_in, last_in, waves_in, turns_in, mix_in, full_in, plain_in)
+    tables_at = (fa, last, waves, turns, mix, full, plain)
+
+    def table(n):
+        return pltpu.make_async_copy(tables_in[n], tables_at[n], table_sem.at[n])
 
     def cube_part(part):
-        return pltpu.make_async_copy(cube.at[rows_of(part)], back.at[rows_of(part)], in_sem.at[part])
+        source = cube.at[:, part_rows(part), :]
+        return pltpu.make_async_copy(source, back.at[:, part_rows(part), :], in_sem.at[part])
 
     def out_part(part):
-        return pltpu.make_async_copy(sent.at[rows_of(part)], tiles.at[rows_of(part)], out_sem.at[part])
+        channels = pl.ds(part * BLOCK, BLOCK)
+        return pltpu.make_async_copy(sent.at[channels], tiles.at[channels], out_sem.at[part])
+
+    def home(row):
+        return columns(back, row, me) if row < ROWS - 1 else columns(final, 0, me)
 
     def own_go(row):
         return pltpu.make_async_copy(columns(sent, row, me), got.at[row, me], own_sem.at[row])
 
     def own_home(row):
-        return pltpu.make_async_copy(got.at[row, me], columns(back, row, me), own_sem.at[ROWS + row])
-
-    @pl.loop(0, BLOCKS)
-    def _(part):
+        return pltpu.make_async_copy(got.at[row, me], home(row), own_sem.at[ROWS + row])
+
+    for part in range(PARTS):
         cube_part(part).start()
-
+    for n in range(len(tables_in)):
+        table(n).start()
     make_marks(flags, marks)
 
-    @pl.loop(0, BLOCKS)
+    @pl.loop(0, PARTS)
     def _(part):
         cube_part(part).wait()
         widen(back, work, part)
+        for q in range(4):
+            turn_in(0, part * 4 + q, work, marks, sent)
 
     for row in range(ROWS):
-        def make(block):
+        def beside(i):
             for q in range(3):
-                turn_in(row, block * 3 + q, work, marks, sent)
-
-        exchange(row, make, lambda d: columns(sent, row, d), got.at[row, me], go_send, go_recv)
+                turn_in(row + 1, i * 3 + q, work, marks, sent)
+
         own_go(row).start()
-
+        exchange(
+            row, lambda d: columns(sent, row, d), got.at[row, me], go_send, go_recv, beside if row < ROWS - 1 else None
+        )
+
+    for n in range(len(tables_in)):
+        table(n).wait()
     make_gain(line, gain)
     make_taps(width, taps)
     make_matrices(gain, waves, turns, hs, mats)
@@ -476,10 +503,13 @@
         shown[row] = fit_row(z, mix, chol, cl)
         filter_row(z, cl, fw, mats)
         channels_row(xs, z, last)
-        exchange(
-            row, lambda i: pack_block(rows, i, xs), lambda d: got.at[row, d], columns(back, row, me), home_send, home_recv
-        )
+
+        @pl.loop(0, SIDE // 8)
+        def _(i):
+            pack_block(rows, i, xs)
+
         own_home(row).start()
+        exchange(row, lambda d: got.at[row, d], home(row), home_send, home_recv)
         dest = fit_target(row)
 
         @pl.when(dest != me)
@@ -490,14 +520,14 @@
         def _():
             fit_local(row).start()
 
-    for row in range(ROWS):
+    for row in range(ROWS - 1):
         own_home(row).wait()
-        wait_rows(row, back, home_recv)
+        wait_all(row, got, home_recv)
         beam_start(row, back, padded)
         beam_row(row, padded, taps, (flat0, flat1, flat2, flat3), work)
 
     for row in range(ROWS):
-        wait_rows(row, sent, go_send)
+        wait_all(row, got, go_send)
 
     @pl.loop(0, BLOCKS)
     def _(part):
@@ -526,6 +556,8 @@
     for slot in range(ROWS):
         continuum[slot * OWN : (slot + 1) * OWN, :] = gathered[slot]
     continuum[ROWS * OWN :, :] = jnp.zeros((2 * SIDE - ROWS * OWN, SIDE), F32)
+    own_home(ROWS - 1).wait()
+    wait_all(ROWS - 1, got, home_recv)
     for row in range(ROWS):
         wait_all(row, got, home_send)
 
@@ -534,19 +566,61 @@
         out_part(part).wait()
 
 
-def leave_kernel(tiles, coefs, restored, continuum, buffer, in_sem, out_sem):
-    def part(i, source, target, sem):
-        rows = pl.ds(pl.multiple_of(i * BLOCK * FLAT, 16), BLOCK * FLAT)
-        return pltpu.make_async_copy(source.at[rows], target.at[rows], sem.at[i])
-
-    for i in range(BLOCKS):
-        part(i, tiles, buffer, in_sem).start()
+def leave_kernel(
+    tiles, final, width, coefs, restored, continuum,
+    landing, leave, last_row, padded, flat0, flat1, flat2, flat3, work, taps, in_sem, out_sem, row_sem,
+):
+    def in_part(part):
+        rows = part_rows(part)
+        return pltpu.make_async_copy(tiles.at[:, rows, :], landing.at[:, rows, :], in_sem.at[part])
+
+    def out_part(part):
+        rows = part_rows(part)
+        return pltpu.make_async_copy(leave.at[:, rows, :], restored.at[:, rows, :], out_sem.at[part])
+
+    def row_part(n):
+        slabs = pl.ds(n * 8, 8)
+        return pltpu.make_async_copy(final.at[slabs], last_row.at[slabs], row_sem.at[n])
+
+    for n in range(4):
+        row_part(n).start()
+    for part in range(PARTS):
+        in_part(part).start()
+    make_taps(width, taps)
     continuum[...] = coefs[...].T[:NBASIS, : ROWS * OWN]
-    for i in range(BLOCKS):
-        part(i, tiles, buffer, in_sem).wait()
-        part(i, buffer, restored, out_sem).start()
-    for i in range(BLOCKS):
-        part(i, buffer, restored, out_sem).wait()
+    for n in range(4):
+        row_part(n).wait()
+    beam_start(0, last_row, padded)
+    flats = (flat0, flat1, flat2, flat3)
+
+    @pl.loop(0, PARTS)
+    def _(part):
+        for q, flat in enumerate(flats):
+            beam_tile(0, part * 4 + q, padded, taps, flat, None)
+        in_part(part).wait()
+
+        @pl.loop(0, SIDE // 8)
+        def _(i):
+            for k in range(8):
+                c = i * 8 + k
+                value = landing[c, part_rows(part), :].astype(F32)
+                work[pl.ds(pl.multiple_of(c * (PART + 8), 8), PART), :] = value
+
+        for q, flat in enumerate(flats):
+            work[pl.ds(q * ROWS + ROWS - 1, SIDE, stride=PART + 8), :] = flat[...].T
+
+        @pl.loop(0, SIDE // 8)
+        def _(i):
+            for k in range(8):
+                c = i * 8 + k
+                value = work[pl.ds(pl.multiple_of(c * (PART + 8), 8), PART), :]
+                leave[c, part_rows(part), :] = value.astype(BF)
+
+        out_part(part).start()
+
+    @pl.loop(0, PARTS)
+    def _(part):
+        out_part(part).wait()
 
 
 def params(**more):
@@ -554,32 +628,34 @@
 
 
 def body(cube, flags, line_gain, beam_width):
-    tab = {k: jnp.asarray(v) for k, v in tables().items()}
-    line = jnp.pad(line_gain, (0, HROWS * SIDE - line_gain.shape[0])).reshape(HROWS, SIDE)
+    tab = tables()
     names = ("fa", "last", "waves", "turns", "mix", "full", "plain")
-    ins = [line, beam_width[None, :]] + [tab[n] for n in names]
+    ins = [jnp.asarray(tab[n]) for n in names]
+    width = beam_width[None, :]
     dma = pltpu.SemaphoreType.DMA
     vmem = pltpu.VMEM
-    flat = cube.reshape(SIDE, ROWS, TILES, SIDE).transpose(0, 2, 1, 3).reshape(SIDE * FLAT, SIDE)
-    tiles, coefs = pl.pallas_call(
+    hbm = pl.BlockSpec(memory_space=pl.ANY)
+    near = pl.BlockSpec(memory_space=vmem)
+    slabs = (SIDE, FLAT, SIDE)
+    row_slabs = (NPIX // FLAT, FLAT, SIDE)
+    flat_tile = [vmem((SIDE, SIDE), F32)] * 4
+    flat = cube.reshape(SIDE, ROWS, TILES, SIDE).transpose(0, 2, 1, 3).reshape(slabs)
+    tiles, final, coefs = pl.pallas_call(
         strip_kernel,
-        in_specs=[pl.BlockSpec(memory_space=pl.ANY), pl.BlockSpec(memory_space=pltpu.SMEM)]
-        + [pl.BlockSpec(memory_space=vmem)] * len(ins),
-        out_specs=[pl.BlockSpec(memory_space=pl.ANY), pl.BlockSpec(memory_space=vmem)],
+        in_specs=[hbm, pl.BlockSpec(memory_space=pltpu.SMEM), near, near] + [hbm] * len(ins),
+        out_specs=[hbm, hbm, near],
         out_shape=[
-            jax.ShapeDtypeStruct((SIDE * FLAT, SIDE), BF),
+            jax.ShapeDtypeStruct(slabs, BF),
+            jax.ShapeDtypeStruct(row_slabs, BF),
             jax.ShapeDtypeStruct((2 * SIDE, SIDE), F32),
         ],
         scratch_shapes=[
             vmem((SIDE * REACH, SIDE), F32),
-            vmem((ROWS * NPIX, SIDE), BF),
+            vmem(slabs, BF),
             vmem((ROWS, NDEV, OWN, SIDE), BF),
-            vmem((ROWS * NPIX, SIDE), BF),
+            vmem(slabs, BF),
             vmem((NPIX + 2 * HALF, SIDE), F32),
-            vmem((SIDE, SIDE), F32),
-            vmem((SIDE, SIDE), F32),
-            vmem((SIDE, SIDE), F32),
-            vmem((SIDE, SIDE), F32),
+            *flat_tile,
             vmem((8, SIDE), F32),
             vmem((HALF + 1, 8, SIDE), F32),
             vmem((HROWS, SIDE), F32),
@@ -592,8 +668,10 @@
             vmem((NBASIS * NBASIS, 8, SIDE), F32),
             vmem((ROWS, OWN, SIDE), F32),
             vmem((ROWS, OWN, SIDE), F32),
+            *[vmem(t.shape, t.dtype) for t in ins],
+            dma((PARTS,)),
             dma((BLOCKS,)),
-            dma((BLOCKS,)),
+            dma((len(ins),)),
             dma((ROWS,)),
             dma((ROWS,)),
             dma((ROWS,)),
@@ -603,18 +681,29 @@
             dma((ROWS,)),
         ],
         compiler_params=params(has_side_effects=True),
-    )(flat, flags, *ins)
+    )(flat, flags, line_gain, width, *ins)
     restored, continuum = pl.pallas_call(
         leave_kernel,
-        in_specs=[pl.BlockSpec(memory_space=pl.ANY), pl.BlockSpec(memory_space=vmem)],
-        out_specs=[pl.BlockSpec(memory_space=pl.ANY), pl.BlockSpec(memory_space=vmem)],
+        in_specs=[hbm, hbm, near, near],
+        out_specs=[hbm, near],
         out_shape=[
-            jax.ShapeDtypeStruct((SIDE * FLAT, SIDE), BF),
+            jax.ShapeDtypeStruct(slabs, BF),
             jax.ShapeDtypeStruct((NBASIS, ROWS * OWN), F32),
         ],
-        scratch_shapes=[vmem((SIDE * FLAT, SIDE), BF), dma((BLOCKS,)), dma((BLOCKS,))],
+        scratch_shapes=[
+            vmem(slabs, BF),
+            vmem(slabs, BF),
+            vmem(row_slabs, BF),
+            vmem((NPIX + 2 * HALF, SIDE), F32),
+            *flat_tile,
+            vmem((SIDE * (PART + 8), SIDE), F32),
+            vmem((HALF + 1, 8, SIDE), F32),
+            dma((PARTS,)),
+            dma((PARTS,)),
+            dma((4,)),
+        ],
         compiler_params=params(),
-    )(tiles, coefs)
+    )(tiles, final, width, coefs)
     restored = restored.reshape(SIDE, TILES, ROWS, SIDE).transpose(0, 2, 1, 3).reshape(SIDE, ROWS, NPIX)
     return (restored, continuum)
 

time: 213 us -> 177 us (0.83)
  the two profiles are of different devices: /device:TPU:4 before, /device:TPU:1 now
where the time goes in v6:
time: 177 us
  Pallas kernels  176 us (99%)
    pallas_call x1, Pallas kernels, body(): pl.pallas_call(strip_kernel, in_specs=[hbm, pl.BlockSpec(memory_space=plt...  162 us
    pallas_call x1, Pallas kernels, body(): pl.pallas_call(leave_kernel, in_specs=[hbm, hbm, near, near], out_specs=[...  14.5 us

profile of v6, /device:TPU:1, one launch (start us, length us, event | category | flops | bytes accessed | tf_op | source)
XLA Modules:
  0.0 177.0 jit_solution(6520430191121632347)
XLA Ops:
  0.6 161.8 %shard_map.122 = (bf16[128,192,128]{2,1,0:T(8,128)(2,1)}, bf16[32,192,128]{2,1,0:T(8,128)(2,1)}, f32[256,128]{1,0:T(8,128)}) custom-call(bf16[128,192,128]{2,1,0:T(8,128)(2,1)} %bitcast.11, s32[8]{0:T(128)} %flags.1, f32[8193]{0:T(1024)} %line.1, f32[1,128]{1,0:T(1,128)} %bitcast.12, bf16[144,256]{1,0:T(8,128)(2,1)} %constant.14.clone.fa_in, ...), custom_call_target="tpu_custom_call" | custom-call | tf_op jit(solution)/shard_map/pallas_call | solution.py:643
  162.4 14.5 %shard_map.123 = (bf16[128,192,128]{2,1,0:T(8,128)(2,1)}, f32[6,192]{1,0:T(8,128)}) custom-call(bf16[128,192,128]{2,1,0:T(8,128)(2,1)} %get-tuple-element.7.tiles, bf16[32,192,128]{2,1,0:T(8,128)(2,1)} %get-tuple-element.8.final, f32[1,128]{1,0:T(1,128)} %bitcast.13, f32[256,128]{1,0:T(8,128)} %get-tuple-element.9.coefs), custom_call_target="tpu_custom_call" | custom-call | tf_op jit(solution)/shard_map/pallas_call | solution.py:685

commit v7 on v6

--- a/solution.py
+++ b/solution.py
@@ -279,9 +279,10 @@
     wide, narrow, _ = place()
     x, y = lax.div(wide, 8), lax.rem(wide, 4)
     z = lax.rem(lax.div(wide, 4), 2) * 2 + lax.div(narrow, 2)
-    x = lax.rem(x + i + j, 4)
-    y = lax.rem(y + (i // 4 if isinstance(i, int) else lax.div(i, 4)) + j // 2, 4)
-    z = lax.rem(z + j % 4, 4)
+    step = (0, 2, 1, 3)[j % 4]
+    x = lax.rem(x + step, 4)
+    y = lax.rem(y + step + i % 4 if isinstance(i, int) else y + step + lax.rem(i, 4), 4)
+    z = lax.rem(z + step + (i // 4 if isinstance(i, int) else lax.div(i, 4)), 4)
     core = lax.rem(lax.rem(narrow, 2) + j // 4, 2)
     return (x * 2 + lax.div(z, 2)) * 4 + y, lax.rem(z, 2) * 2 + core
 
@@ -321,10 +322,10 @@
 
 
 def widen(landing, work, part):
-    @pl.loop(0, SIDE // 8)
+    @pl.loop(0, SIDE // 32)
     def _(i):
-        for k in range(8):
-            c = i * 8 + k
+        for k in range(32):
+            c = i * 32 + k
             value = landing[c, part_rows(part), :]
             work[pl.ds(pl.multiple_of(c * REACH + part * PART, 8), PART), :] = value.astype(F32)
 
@@ -599,20 +600,20 @@
             beam_tile(0, part * 4 + q, padded, taps, flat, None)
         in_part(part).wait()
 
-        @pl.loop(0, SIDE // 8)
+        @pl.loop(0, SIDE // 32)
         def _(i):
-            for k in range(8):
-                c = i * 8 + k
+            for k in range(32):
+                c = i * 32 + k
                 value = landing[c, part_rows(part), :].astype(F32)
                 work[pl.ds(pl.multiple_of(c * (PART + 8), 8), PART), :] = value
 
         for q, flat in enumerate(flats):
             work[pl.ds(q * ROWS + ROWS - 1, SIDE, stride=PART + 8), :] = flat[...].T
 
-        @pl.loop(0, SIDE // 8)
+        @pl.loop(0, SIDE // 32)
         def _(i):
-            for k in range(8):
-                c = i * 8 + k
+            for k in range(32):
+                c = i * 32 + k
                 value = work[pl.ds(pl.multiple_of(c * (PART + 8), 8), PART), :]
                 leave[c, part_rows(part), :] = value.astype(BF)
 

time: 177 us -> 180 us (1.017); the launches traced: 177 us -> 177 us
  no operation moved by 1% of the time
where the time goes in v7:
time: 180 us; the launch traced here: 177 us
  Pallas kernels  176 us (98%)
    pallas_call x1, Pallas kernels, body(): pl.pallas_call(strip_kernel, in_specs=[hbm, pl.BlockSpec(memory_space=plt...  163 us
    pallas_call x1, Pallas kernels, body(): pl.pallas_call(leave_kernel, in_specs=[hbm, hbm, near, near], out_specs=[...  13.4 us

profile of v7, /device:TPU:1, one launch (start us, length us, event | category | flops | bytes accessed | tf_op | source)
XLA Modules:
  0.0 176.9 jit_solution(8628202796881979561)
XLA Ops:
  0.6 162.9 %shard_map.122 = (bf16[128,192,128]{2,1,0:T(8,128)(2,1)}, bf16[32,192,128]{2,1,0:T(8,128)(2,1)}, f32[256,128]{1,0:T(8,128)}) custom-call(bf16[128,192,128]{2,1,0:T(8,128)(2,1)} %bitcast.11, s32[8]{0:T(128)} %flags.1, f32[8193]{0:T(1024)} %line.1, f32[1,128]{1,0:T(1,128)} %bitcast.12, bf16[144,256]{1,0:T(8,128)(2,1)} %constant.14.clone.fa_in, ...), custom_call_target="tpu_custom_call" | custom-call | tf_op jit(solution)/shard_map/pallas_call | solution.py:644
  163.5 13.4 %shard_map.123 = (bf16[128,192,128]{2,1,0:T(8,128)(2,1)}, f32[6,192]{1,0:T(8,128)}) custom-call(bf16[128,192,128]{2,1,0:T(8,128)(2,1)} %get-tuple-element.7.tiles, bf16[32,192,128]{2,1,0:T(8,128)(2,1)} %get-tuple-element.8.final, f32[1,128]{1,0:T(1,128)} %bitcast.13, f32[256,128]{1,0:T(8,128)} %get-tuple-element.9.coefs), custom_call_target="tpu_custom_call" | custom-call | tf_op jit(solution)/shard_map/pallas_call | solution.py:686

commit v8 on v7

--- a/solution.py
+++ b/solution.py
@@ -135,7 +135,7 @@
         chol[i * NBASIS + j] = value
 
 
-def make_matrices(gain, waves, turns, hs, mats):
+def make_matrices(gain, waves, turns, hs, mats, send=None):
     def exact(a, b):
         return jnp.dot(a, b, preferred_element_type=F32, precision=lax.Precision.HIGHEST)
 
@@ -144,8 +144,7 @@
     hs[0] = real * turns[0] - imag * turns[1]
     hs[1] = real * turns[1] + imag * turns[0]
 
-    @pl.loop(0, KEPT)
-    def _(k):
+    def one(k):
         for part in range(2):
             rows = jnp.broadcast_to(hs[part, pl.ds(k, 1), :], (SIDE, 2 * SIDE))
             matrix = pltpu.roll(rows, 0, 1, stride=1, stride_axis=0)[:, SIDE:]
@@ -155,6 +154,12 @@
             if part == 1:
                 mats[k, 4] = -hi
                 mats[k, 5] = -lo
+
+    def turn(t):
+        for j in range(BINS):
+            one(t * BINS + j)
+
+    beside_bins(send, turn)
 
 
 def fit_row(z, mix, chol, cl):
@@ -206,7 +211,7 @@
                 z[pl.ds(base, 2 * HROWS), :] = res[:, q * SIDE : (q + 1) * SIDE]
 
 
-def filter_row(z, cl, fw, mats):
+def filter_row(z, cl, fw, mats, send=None):
     def rows(k):
         return pl.ds(k, OWN, stride=ZSTEP), pl.ds(k + HROWS, OWN, stride=ZSTEP)
 
@@ -227,8 +232,7 @@
         both = dot(jnp.concatenate([hi, lo], axis=0), matrix(0))
         return both[:OWN] + both[OWN:] + dot(hi, matrix(1))
 
-    @pl.loop(0, KEPT // BINS)
-    def _(i):
+    def turn(i):
         values = []
         for j in range(BINS):
             real, imag = rows(i * BINS + j)
@@ -238,6 +242,8 @@
             real, imag = rows(i * BINS + j)
             z[real, :] = value[:, :SIDE]
             z[imag, :] = value[:, SIDE:]
+
+    beside_bins(send, turn)
 
 
 def channels_row(xs, z, last):
@@ -287,7 +293,7 @@
     return (x * 2 + lax.div(z, 2)) * 4 + y, lax.rem(z, 2) * 2 + core
 
 
-def exchange(row, source, target, send_sem, recv_sem, beside=None):
+def sender(row, source, target, send_sem, recv_sem):
     def send(i, j):
         wide, narrow = partner(i, j)
         pltpu.make_async_remote_copy(
@@ -299,6 +305,10 @@
             device_id_type=pl.DeviceIdType.MESH,
         ).start()
 
+    return send
+
+
+def send_all(send, beside=None):
     @pl.loop(1, 16)
     def _(i):
         for j in range(8):
@@ -310,6 +320,20 @@
         send(0, j)
     if beside is not None:
         beside(0)
+
+
+def beside_bins(send, work):
+    @pl.loop(0, KEPT // BINS)
+    def _(t):
+        if send is not None:
+            for d in range(1, 4):
+                for j in range(8):
+                    send(3 * t + d, j)
+        work(t)
+
+    if send is not None:
+        for j in range(1, 8):
+            send(0, j)
 
 
 def wait_all(row, buffer, sem):
@@ -466,15 +490,15 @@
                 turn_in(row + 1, i * 3 + q, work, marks, sent)
 
         own_go(row).start()
-        exchange(
-            row, lambda d: columns(sent, row, d), got.at[row, me], go_send, go_recv, beside if row < ROWS - 1 else None
-        )
+        go = sender(row, lambda d, row=row: columns(sent, row, d), got.at[row, me], go_send, go_recv)
+        if row < ROWS - 1:
+            send_all(go, beside)
 
     for n in range(len(tables_in)):
         table(n).wait()
     make_gain(line, gain)
     make_taps(width, taps)
-    make_matrices(gain, waves, turns, hs, mats)
+    make_matrices(gain, waves, turns, hs, mats, go)
 
     def fit_target(row):
         return row * (NDEV // ROWS) + me // ROWS
@@ -493,6 +517,7 @@
     def fit_local(row):
         return pltpu.make_async_copy(shown.at[row], gathered.at[me % ROWS], fit_send.at[row])
 
+    back_home = None
     for row in range(ROWS):
         own_go(row).wait()
         wait_all(row, got, go_recv)
@@ -502,7 +527,7 @@
             fit_setup(xs, full, plain, fw, chol)
         spectrum_row(xs, z, fa)
         shown[row] = fit_row(z, mix, chol, cl)
-        filter_row(z, cl, fw, mats)
+        filter_row(z, cl, fw, mats, back_home)
         channels_row(xs, z, last)
 
         @pl.loop(0, SIDE // 8)
@@ -510,7 +535,9 @@
             pack_block(rows, i, xs)
 
         own_home(row).start()
-        exchange(row, lambda d: got.at[row, d], home(row), home_send, home_recv)
+        back_home = sender(row, lambda d, row=row: got.at[row, d], home(row), home_send, home_recv)
+        if row == ROWS - 1:
+            send_all(back_home)
         dest = fit_target(row)
 
         @pl.when(dest != me)

time: 180 us -> 180 us (level)
  no operation moved by 1% of the time
where the time goes in v8:
time: 180 us; the launch traced here: 177 us
  Pallas kernels  176 us (98%)
    pallas_call x1, Pallas kernels, body(): pl.pallas_call(strip_kernel, in_specs=[hbm, pl.BlockSpec(memory_space=plt...  163 us
    pallas_call x1, Pallas kernels, body(): pl.pallas_call(leave_kernel, in_specs=[hbm, hbm, near, near], out_specs=[...  13.4 us

profile of v8, /device:TPU:1, one launch (start us, length us, event | category | flops | bytes accessed | tf_op | source)
XLA Modules:
  0.0 176.9 jit_solution(16466713084593976139)
XLA Ops:
  0.6 162.9 %shard_map.122 = (bf16[128,192,128]{2,1,0:T(8,128)(2,1)}, bf16[32,192,128]{2,1,0:T(8,128)(2,1)}, f32[256,128]{1,0:T(8,128)}) custom-call(bf16[128,192,128]{2,1,0:T(8,128)(2,1)} %bitcast.11, s32[8]{0:T(128)} %flags.1, f32[8193]{0:T(1024)} %line.1, f32[1,128]{1,0:T(1,128)} %bitcast.12, bf16[144,256]{1,0:T(8,128)(2,1)} %constant.14.clone.fa_in, ...), custom_call_target="tpu_custom_call" | custom-call | tf_op jit(solution)/shard_map/pallas_call | solution.py:671
  163.5 13.4 %shard_map.123 = (bf16[128,192,128]{2,1,0:T(8,128)(2,1)}, f32[6,192]{1,0:T(8,128)}) custom-call(bf16[128,192,128]{2,1,0:T(8,128)(2,1)} %get-tuple-element.7.tiles, bf16[32,192,128]{2,1,0:T(8,128)(2,1)} %get-tuple-element.8.final, f32[1,128]{1,0:T(1,128)} %bitcast.13, f32[256,128]{1,0:T(8,128)} %get-tuple-element.9.coefs), custom_call_target="tpu_custom_call" | custom-call | tf_op jit(solution)/shard_map/pallas_call | solution.py:713

commit v9 on v8

--- a/solution.py
+++ b/solution.py
@@ -439,6 +439,8 @@
         for q, flat in enumerate(flats):
             tile = i * len(flats) + q
             work[pl.ds(tile * ROWS + row, SIDE, stride=REACH), :] = flat[...].T
+            if row == ROWS - 2:
+                work[pl.ds(tile * ROWS + ROWS - 1, SIDE, stride=REACH), :] = jnp.zeros((SIDE, SIDE), F32)
 
 
 def strip_kernel(
@@ -616,34 +618,34 @@
         in_part(part).start()
     make_taps(width, taps)
     continuum[...] = coefs[...].T[:NBASIS, : ROWS * OWN]
+    work[...] = jnp.zeros(work.shape, F32)
+    padded[0:HALF, :] = jnp.zeros((HALF, SIDE), F32)
+    padded[HALF + NPIX : NPIX + 2 * HALF, :] = jnp.zeros((HALF, SIDE), F32)
     for n in range(4):
         row_part(n).wait()
-    beam_start(0, last_row, padded)
+
+        @pl.loop(n * 8, n * 8 + 8)
+        def _(i):
+            at = pl.multiple_of(i * FLAT + HALF, 8)
+            padded[pl.ds(at, FLAT), :] = last_row[i].astype(F32)
+
     flats = (flat0, flat1, flat2, flat3)
+
+    def beams(part):
+        for q, flat in enumerate(flats):
+            beam_tile(0, part * 4 + q, padded, taps, flat, None)
+
+    beams(0)
 
     @pl.loop(0, PARTS)
     def _(part):
-        for q, flat in enumerate(flats):
-            beam_tile(0, part * 4 + q, padded, taps, flat, None)
         in_part(part).wait()
-
-        @pl.loop(0, SIDE // 32)
-        def _(i):
-            for k in range(32):
-                c = i * 32 + k
-                value = landing[c, part_rows(part), :].astype(F32)
-                work[pl.ds(pl.multiple_of(c * (PART + 8), 8), PART), :] = value
-
         for q, flat in enumerate(flats):
             work[pl.ds(q * ROWS + ROWS - 1, SIDE, stride=PART + 8), :] = flat[...].T
-
-        @pl.loop(0, SIDE // 32)
-        def _(i):
-            for k in range(32):
-                c = i * 32 + k
-                value = work[pl.ds(pl.multiple_of(c * (PART + 8), 8), PART), :]
-                leave[c, part_rows(part), :] = value.astype(BF)
-
+        beams(lax.min(part + 1, PARTS - 1))
+        for c in range(SIDE):
+            value = work[c * (PART + 8) : c * (PART + 8) + PART, :].astype(BF)
+            leave[c, part_rows(part), :] = landing[c, part_rows(part), :] + value
         out_part(part).start()
 
     @pl.loop(0, PARTS)

time: 180 us -> 180 us (level)
  no operation moved by 1% of the time
where the time goes in v9:
time: 180 us; the launch traced here: 177 us
  Pallas kernels  176 us (98%)
    pallas_call x1, Pallas kernels, body(): pl.pallas_call(strip_kernel, in_specs=[hbm, pl.BlockSpec(memory_space=plt...  163 us
    pallas_call x1, Pallas kernels, body(): pl.pallas_call(leave_kernel, in_specs=[hbm, hbm, near, near], out_specs=[...  12.8 us

profile of v9, /device:TPU:1, one launch (start us, length us, event | category | flops | bytes accessed | tf_op | source)
XLA Modules:
  0.0 176.8 jit_solution(1469080407094240612)
XLA Ops:
  0.6 163.2 %shard_map.122 = (bf16[128,192,128]{2,1,0:T(8,128)(2,1)}, bf16[32,192,128]{2,1,0:T(8,128)(2,1)}, f32[256,128]{1,0:T(8,128)}) custom-call(bf16[128,192,128]{2,1,0:T(8,128)(2,1)} %bitcast.11, s32[8]{0:T(128)} %flags.1, f32[8193]{0:T(1024)} %line.1, f32[1,128]{1,0:T(1,128)} %bitcast.12, bf16[144,256]{1,0:T(8,128)(2,1)} %constant.14.clone.fa_in, ...), custom_call_target="tpu_custom_call" | custom-call | tf_op jit(solution)/shard_map/pallas_call | solution.py:673
  163.8 12.8 %shard_map.123 = (bf16[128,192,128]{2,1,0:T(8,128)(2,1)}, f32[6,192]{1,0:T(8,128)}) custom-call(bf16[128,192,128]{2,1,0:T(8,128)(2,1)} %get-tuple-element.7.tiles, bf16[32,192,128]{2,1,0:T(8,128)(2,1)} %get-tuple-element.8.final, f32[1,128]{1,0:T(1,128)} %bitcast.13, f32[256,128]{1,0:T(8,128)} %get-tuple-element.9.coefs), custom_call_target="tpu_custom_call" | custom-call | tf_op jit(solution)/shard_map/pallas_call | solution.py:715
